TPU v7x, 256 devices: a whole 4x4x8 slice. The times are simulated.
256 devices in a mesh: head: 8 (over z), outer: 4 (over y_lo, core), inner: 8 (over y_hi, x).
Axes of the slice: x: 4, y: 4 (y_hi: 2, y_lo: 2; y = y_hi * 2 + y_lo), z: 8, core: 2. Of those that a mesh axis runs over, the one named last changes fastest.
Arguments:
- queries: bfloat16 [4, 3072, 4096], P('outer', ('inner', 'head')), may hold values from -90 to 90
- keys: bfloat16 [4, 3072, 4096], P('outer', ('inner', 'head')), may hold values from -3 to 3
- values: bfloat16 [4, 3072, 4096], P('outer', ('inner', 'head')), may hold values from -6 to 6
- out_grad: bfloat16 [4, 3072, 4096], P('outer', ('inner', 'head')), may hold values from -6 to 6
- outputs: bfloat16 [4, 3072, 4096], P('outer', ('inner', 'head')), may hold values from -3 to 3
- doc_ids: int32 [4, 24], P('outer'), may hold values from 0 to 7, never falling along the last dimension, each value on 1 to 12 neighbouring positions
- block_order: int32 [4, 24], P('outer'), may hold values from 0 to 23, each once within a row
Outputs:
- query_grad: bfloat16 [4, 3072, 4096], P('outer', ('inner', 'head'))
- key_grad: bfloat16 [4, 3072, 4096], P('outer', ('inner', 'head'))
- value_grad: bfloat16 [4, 3072, 4096], P('outer', ('inner', 'head'))
Inputs may be any that keep to these rules, and one draw needn't show every extreme that they name: `doc_ids`: never falling along a window's sequence; in each window one document spans 12 blocks. `block_order`: each sequence block of a window appears once in its row.
All inputs are finite; a program needn't handle non-finite values.
Results may differ from a plain program's by a relative error of at most 0.0049.
Values may be sent and summed in bfloat16 or wider, within the bound.
No kernel may reach another device: no remote copies, remote signals or barrier semaphores. Data moves between devices by JAX's collectives and lax.ppermute only.
A program may use at most 64 MiB of HBM per device.

v0:
```python
import math

import jax
import jax.numpy as jnp
from jax import lax
from jax.sharding import PartitionSpec as P

HD = 128
BLOCK = 128


NEG_FILL = -1e30


def passed_along(value, axis, steps):
    count = lax.axis_size(axis)
    pairs = [(source, (source + steps) % count) for source in range(count)]
    return lax.ppermute(value, axis, pairs)


def row_meta(first_row, count, doc_ids, block_order):
    stored_rows = first_row + lax.iota(jnp.int32, count)
    table_index = lax.iota(jnp.int32, block_order.shape[0])
    seq_block = jnp.sum(
        jnp.where((stored_rows // BLOCK)[:, None] == table_index[None, :], block_order[None, :], 0),
        axis=1,
    )
    document = jnp.sum(
        jnp.where(seq_block[:, None] == table_index[None, :], doc_ids[None, :], 0), axis=1
    )
    return (seq_block * BLOCK + stored_rows % BLOCK, document)


def visible(query_meta, key_meta):
    return (key_meta[0][None, :] <= query_meta[0][:, None]) & (
        key_meta[1][None, :] == query_meta[1][:, None]
    )


def as_heads(matrix):
    return matrix.reshape(matrix.shape[0], -1, HD)


def score_tile(query_heads, key_heads, allowed):
    scores = jnp.einsum(
        "qhd,khd->hqk", query_heads, key_heads, preferred_element_type=jnp.float32
    ) * (1.0 / math.sqrt(HD))
    return jnp.where(allowed[None], scores, NEG_FILL)


def tile_grads(query_heads, grad_heads, log_total, out_dot, key_heads, value_heads, allowed):
    score_scale = 1.0 / math.sqrt(HD)
    scores = score_tile(query_heads, key_heads, allowed)
    weights = jnp.where(allowed[None], jnp.exp(scores - log_total[:, :, None]), 0.0)
    weights_low = weights.astype(jnp.bfloat16)
    value_part = jnp.einsum(
        "hqk,qhd->khd", weights_low, grad_heads, preferred_element_type=jnp.float32
    )
    weight_grad = jnp.einsum(
        "qhd,khd->hqk", grad_heads, value_heads, preferred_element_type=jnp.float32
    )
    score_grad = (weights * (weight_grad - out_dot[:, :, None])).astype(jnp.bfloat16)
    query_part = (
        jnp.einsum("hqk,khd->qhd", score_grad, key_heads, preferred_element_type=jnp.float32)
        * score_scale
    )
    key_part = (
        jnp.einsum("hqk,qhd->khd", score_grad, query_heads, preferred_element_type=jnp.float32)
        * score_scale
    )
    return (query_part, key_part, value_part)


def local(queries, keys, values, out_grad, outputs, doc_ids, block_order):
    doc_ids = doc_ids[0]
    block_order = block_order[0]
    cycle_size = lax.axis_size("inner")
    cycle_index = lax.axis_index("inner")
    query_rows, key_rows, value_rows, grad_rows, output_rows = (
        lax.all_to_all(queries[0], "head", split_axis=1, concat_axis=0, tiled=True),
        lax.all_to_all(keys[0], "head", split_axis=1, concat_axis=0, tiled=True),
        lax.all_to_all(values[0], "head", split_axis=1, concat_axis=0, tiled=True),
        lax.all_to_all(out_grad[0], "head", split_axis=1, concat_axis=0, tiled=True),
        lax.all_to_all(outputs[0], "head", split_axis=1, concat_axis=0, tiled=True),
    )
    row_count = query_rows.shape[0]
    width = query_rows.shape[1]
    own_meta = row_meta(cycle_index * row_count, row_count, doc_ids, block_order)
    query_heads = as_heads(query_rows)
    grad_heads = as_heads(grad_rows)
    head_count = query_heads.shape[1]
    out_dot = jnp.sum(
        grad_heads.astype(jnp.float32) * as_heads(output_rows).astype(jnp.float32), axis=2
    ).T
    start_stats = (
        jnp.full((head_count, row_count), NEG_FILL, jnp.float32),
        jnp.zeros((head_count, row_count), jnp.float32),
    )
    key_piece = lax.all_gather(key_rows, "inner", axis=0, tiled=True)
    allowed = visible(own_meta, row_meta(jnp.int32(0), key_piece.shape[0], doc_ids, block_order))
    scores = score_tile(query_heads, as_heads(key_piece), allowed)
    highest = jnp.maximum(start_stats[0], jnp.max(scores, axis=2))
    weights = jnp.where(allowed[None], jnp.exp(scores - highest[:, :, None]), 0.0)
    highest, totals = (highest, jnp.sum(weights, axis=2))
    log_total = highest + jnp.log(totals)

    def key_visit(hop_index, query_grad, key_pair, grad_pair):
        owner_index = (cycle_index - hop_index) % cycle_size
        allowed = visible(
            own_meta, row_meta(owner_index * row_count, row_count, doc_ids, block_order)
        )
        running = (query_grad, grad_pair[0], grad_pair[1])
        pieces = tile_grads(
            query_heads,
            grad_heads,
            log_total,
            out_dot,
            as_heads(key_pair[0]),
            as_heads(key_pair[1]),
            allowed,
        )
        return (
            running[0] + pieces[0],
            running[1] + pieces[1].reshape(running[1].shape),
            running[2] + pieces[2].reshape(running[2].shape),
        )

    def pass_key_grads(grad_pair):
        return passed_along((grad_pair[0], grad_pair[1]), "inner", 1)

    zero_pair = (
        jnp.zeros((row_count, width), jnp.float32),
        jnp.zeros((row_count, width), jnp.float32),
    )

    def key_step(hop_index, carried):
        query_grad, key_pair, grad_pair = carried
        query_grad, key_grad, value_grad = key_visit(hop_index, query_grad, key_pair, grad_pair)
        key_pair = passed_along((key_pair[0], key_pair[1]), "inner", 1)
        return (query_grad, key_pair, pass_key_grads((key_grad, value_grad)))

    carried = (jnp.zeros(query_heads.shape, jnp.float32), (key_rows, value_rows), zero_pair)
    query_grad, key_pair, grad_pair = lax.fori_loop(0, cycle_size - 1, key_step, carried)
    query_grad, key_grad, value_grad = key_visit(cycle_size - 1, query_grad, key_pair, grad_pair)
    key_grad, value_grad = pass_key_grads((key_grad, value_grad))
    query_grad = query_grad.reshape(row_count, width)
    query_back, key_back, value_back = (
        lax.all_to_all(
            query_grad.astype(jnp.bfloat16), "head", split_axis=0, concat_axis=1, tiled=True
        ),
        lax.all_to_all(
            key_grad.astype(jnp.bfloat16), "head", split_axis=0, concat_axis=1, tiled=True
        ),
        lax.all_to_all(
            value_grad.astype(jnp.bfloat16), "head", split_axis=0, concat_axis=1, tiled=True
        ),
    )
    return (query_back[None], key_back[None], value_back[None])


def solution(mesh):
    return jax.shard_map(
        local,
        mesh=mesh,
        in_specs=(
            P("outer", ("inner", "head"), None),
            P("outer", ("inner", "head"), None),
            P("outer", ("inner", "head"), None),
            P("outer", ("inner", "head"), None),
            P("outer", ("inner", "head"), None),
            P("outer", None),
            P("outer", None),
        ),
        out_specs=(
            P("outer", ("inner", "head"), None),
            P("outer", ("inner", "head"), None),
            P("outer", ("inner", "head"), None),
        ),
        check_vma=False,
    )
```

profile of v0, /device:TPU:32, one launch (start us, length us, event | category | flops | bytes accessed | tf_op | source)
XLA Modules:
  0.0 682.0 jit_solution(5627772023102324517)
XLA Ops:
  8.5 21.7 %all_to_all.128 = bf16[48,8,512]{2,0,1:T(8,128)(2,1)} all-to-all(bf16[48,8,512]{2,0,1:T(8,128)(2,1)S(1)} %copy.181), channel_id=1, replica_groups=mesh['head'=8,'outer'=4,'inner'=8] {'head'}, dimensions={1} | all-to-all | bytes 786432 | tf_op jit(solution)/shard_map/all_to_all | solution.py:81
  31.3 4.9 all-to-all-start.2
  37.6 10.7 %all-to-all-done.2 = bf16[48,8,512]{2,0,1:T(8,128)(2,1)S(1)} async-done(((bf16[48,8,512]{2,0,1:T(8,128)(2,1)}), bf16[48,8,512]{2,0,1:T(8,128)(2,1)S(1)}, u32[]{:S(2)}, u32[]{:S(2)}) %all-to-all-start.2) | async-done | bytes 393248 | tf_op jit(solution)/shard_map/all_to_all | solution.py:80
  48.3 4.8 all-to-all-start.3
  56.1 7.7 %all-to-all-done.3 = bf16[48,8,512]{2,0,1:T(8,128)(2,1)S(1)} async-done(((bf16[48,8,512]{2,0,1:T(8,128)(2,1)}), bf16[48,8,512]{2,0,1:T(8,128)(2,1)S(1)}, u32[]{:S(2)}, u32[]{:S(2)}) %all-to-all-start.3) | async-done | bytes 393248 | tf_op jit(solution)/shard_map/all_to_all | solution.py:83
  63.8 4.9 all-to-all-start.4
  72.0 6.7 all-to-all-done.4
  78.6 6.0 all-to-all-start.1
  85.5 10.4 %all-gather.2.cloned.1.call-done = bf16[3072,512]{1,0:T(8,128)(2,1)} async-done(((bf16[384,512]{1,0:T(8,128)(2,1)}), bf16[3072,512]{1,0:T(8,128)(2,1)}) %all-gather.2.cloned.1.call-update) | async-done | bytes 3145744 | tf_op jit(solution)/shard_map/all_gather | solution.py:99
  95.9 4.7 copy.184
  100.6 5.7 fusion.15
  106.3 6.3 select_reduce_fusion.2
  115.1 486.0 %while.25 = (s32[]{:T(128)}, f32[384,4,128]{2,0,1:T(8,128)}, bf16[384,512]{1,0:T(8,128)(2,1)}, bf16[384,512]{1,0:T(8,128)(2,1)}, f32[384,512]{0,1:T(8,128)}, /*i...) while((s32[]{:T(128)}, f32[384,4,128]{2,0,1:T(8,128)}, ...), condition=%wide.region_10.11_spmd.clone, body=%wide.region_7.10_spmd.clone.sunk | while | flops 761381376 | bytes 43579492 | solution.py:143
  122.8 2.4 fusion.95
  137.5 42.1 %collective-permute-done = bf16[384,512]{1,0:T(8,128)(2,1)} collective-permute-done((bf16[384,512]{1,0:T(8,128)(2,1)}, bf16[384,512]{1,0:T(8,128)(2,1)}, u32[]{:S(2)}, u32[]{:S(2)}) %collective-permute-start) | collective-permute-done | bytes 393248 | tf_op jit(solution)/shard_map/while/body/eval_jaxpr/ppermute | solution.py:18
  179.6 6.8 collective-permute-done.1
  195.0 2.4 fusion.95
  203.5 3.8 collective-permute-start.1
  207.3 2.6 fusion.94
  210.0 41.8 %collective-permute-done = bf16[384,512]{1,0:T(8,128)(2,1)} collective-permute-done((bf16[384,512]{1,0:T(8,128)(2,1)}, bf16[384,512]{1,0:T(8,128)(2,1)}, u32[]{:S(2)}, u32[]{:S(2)}) %collective-permute-start) | collective-permute-done | bytes 393248 | tf_op jit(solution)/shard_map/while/body/eval_jaxpr/ppermute | solution.py:18
  251.8 5.9 collective-permute-done.1
  274.8 3.8 collective-permute-start.1
  278.6 2.6 fusion.94
  281.2 41.8 %collective-permute-done = bf16[384,512]{1,0:T(8,128)(2,1)} collective-permute-done((bf16[384,512]{1,0:T(8,128)(2,1)}, bf16[384,512]{1,0:T(8,128)(2,1)}, u32[]{:S(2)}, u32[]{:S(2)}) %collective-permute-start) | collective-permute-done | bytes 393248 | tf_op jit(solution)/shard_map/while/body/eval_jaxpr/ppermute | solution.py:18
  323.1 5.0 collective-permute-done.1
  336.6 2.4 fusion.95
  345.1 3.8 collective-permute-start.1
  349.0 2.6 fusion.94
  351.6 41.6 %collective-permute-done = bf16[384,512]{1,0:T(8,128)(2,1)} collective-permute-done((bf16[384,512]{1,0:T(8,128)(2,1)}, bf16[384,512]{1,0:T(8,128)(2,1)}, u32[]{:S(2)}, u32[]{:S(2)}) %collective-permute-start) | collective-permute-done | bytes 393248 | tf_op jit(solution)/shard_map/while/body/eval_jaxpr/ppermute | solution.py:18
  393.2 4.2 collective-permute-done.1
  414.5 3.9 collective-permute-start.1
  418.4 2.6 fusion.94
  421.0 40.7 %collective-permute-done = bf16[384,512]{1,0:T(8,128)(2,1)} collective-permute-done((bf16[384,512]{1,0:T(8,128)(2,1)}, bf16[384,512]{1,0:T(8,128)(2,1)}, u32[]{:S(2)}, u32[]{:S(2)}) %collective-permute-start) | collective-permute-done | bytes 393248 | tf_op jit(solution)/shard_map/while/body/eval_jaxpr/ppermute | solution.py:18
  461.8 4.2 collective-permute-done.1
  483.1 3.9 collective-permute-start.1
  486.9 2.6 fusion.94
  489.5 39.8 %collective-permute-done = bf16[384,512]{1,0:T(8,128)(2,1)} collective-permute-done((bf16[384,512]{1,0:T(8,128)(2,1)}, bf16[384,512]{1,0:T(8,128)(2,1)}, u32[]{:S(2)}, u32[]{:S(2)}) %collective-permute-start) | collective-permute-done | bytes 393248 | tf_op jit(solution)/shard_map/while/body/eval_jaxpr/ppermute | solution.py:18
  529.3 4.2 collective-permute-done.1
  550.6 3.9 collective-permute-start.1
  554.5 2.6 fusion.94
  557.1 38.9 %collective-permute-done = bf16[384,512]{1,0:T(8,128)(2,1)} collective-permute-done((bf16[384,512]{1,0:T(8,128)(2,1)}, bf16[384,512]{1,0:T(8,128)(2,1)}, u32[]{:S(2)}, u32[]{:S(2)}) %collective-permute-start) | collective-permute-done | bytes 393248 | tf_op jit(solution)/shard_map/while/body/eval_jaxpr/ppermute | solution.py:18
  596.0 4.2 collective-permute-done.1
  610.2 7.5 %all-to-all-start.5 = ((bf16[8,48,512]{2,1,0:T(8,128)(2,1)}), bf16[8,48,512]{2,1,0:T(8,128)(2,1)S(1)}, u32[]{:S(2)}, u32[]{:S(2)}) async-start(bf16[8,48,512]{2,1,0:T(8,128)(2,1)} %convert_element_type.59), calls=%async_computation.5 | async-start | bytes 786432 | tf_op jit(solution)/shard_map/all_to_all | solution.py:148
  622.7 11.5 %collective-permute-done.5 = bf16[384,512]{1,0:T(8,128)(2,1)} collective-permute-done((bf16[384,512]{1,0:T(8,128)(2,1)S(1)}, bf16[384,512]{1,0:T(8,128)(2,1)}, u32[]{:S(2)}, u32[]{:S(2)}) %collective-permute-start.5) | collective-permute-done | bytes 393248 | tf_op jit(solution)/shard_map/ppermute | solution.py:18
  634.2 7.2 %all-to-all-start.7 = ((bf16[8,48,512]{2,1,0:T(8,128)(2,1)}), bf16[8,48,512]{2,1,0:T(8,128)(2,1)}, u32[]{:S(2)}, u32[]{:S(2)}) async-start(bf16[8,48,512]{2,1,0:T(8,128)(2,1)} %bitcast.22), calls=%async_computation.7 | async-start | bytes 786432 | tf_op jit(solution)/shard_map/all_to_all | solution.py:154
  644.9 11.5 %collective-permute-done.4 = bf16[384,512]{1,0:T(8,128)(2,1)} collective-permute-done((bf16[384,512]{1,0:T(8,128)(2,1)S(1)}, bf16[384,512]{1,0:T(8,128)(2,1)}, u32[]{:S(2)}, u32[]{:S(2)}) %collective-permute-start.4) | collective-permute-done | bytes 393248 | tf_op jit(solution)/shard_map/ppermute | solution.py:18
  656.3 7.2 %all-to-all-start.6 = ((bf16[8,48,512]{2,1,0:T(8,128)(2,1)}), bf16[8,48,512]{2,1,0:T(8,128)(2,1)S(1)}, u32[]{:S(2)}, u32[]{:S(2)}) async-start(bf16[8,48,512]{2,1,0:T(8,128)(2,1)} %bitcast.18), calls=%async_computation.6 | async-start | bytes 786432 | tf_op jit(solution)/shard_map/all_to_all | solution.py:151
  666.9 7.1 %all-to-all-done.6 = bf16[8,48,512]{2,1,0:T(8,128)(2,1)S(1)} async-done(((bf16[8,48,512]{2,1,0:T(8,128)(2,1)}), bf16[8,48,512]{2,1,0:T(8,128)(2,1)S(1)}, u32[]{:S(2)}, u32[]{:S(2)}) %all-to-all-start.6) | async-done | bytes 393248 | tf_op jit(solution)/shard_map/all_to_all | solution.py:151
  (298 shorter events, 153.1 us)
Async XLA Ops:
  7.2 88.8 %all-gather.2.cloned.1.call-start = ((), (), s32[]{:S(2)}) async-start(), calls=%async_computation.8 | async-start | bytes 3538944 | tf_op jit(solution)/shard_map/all_gather | solution.py:99
  31.3 17.0 %all-to-all-start.2 = ((bf16[48,8,512]{2,0,1:T(8,128)(2,1)}), bf16[48,8,512]{2,0,1:T(8,128)(2,1)S(1)}, u32[]{:S(2)}, u32[]{:S(2)}) async-start(bf16[48,8,512]{2,0,1:T(8,128)(2,1)} %copy.183), calls=%async_computation.2 | async-start | bytes 786432 | tf_op jit(solution)/shard_map/all_to_all | solution.py:80
  48.3 15.5 %all-to-all-start.3 = ((bf16[48,8,512]{2,0,1:T(8,128)(2,1)}), bf16[48,8,512]{2,0,1:T(8,128)(2,1)S(1)}, u32[]{:S(2)}, u32[]{:S(2)}) async-start(bf16[48,8,512]{2,0,1:T(8,128)(2,1)} %copy.187), calls=%async_computation.3 | async-start | bytes 786432 | tf_op jit(solution)/shard_map/all_to_all | solution.py:83
  63.8 14.8 %all-to-all-start.4 = ((bf16[48,8,512]{2,0,1:T(8,128)(2,1)}), bf16[48,8,512]{2,0,1:T(8,128)(2,1)S(1)}, u32[]{:S(2)}, u32[]{:S(2)}) async-start(bf16[48,8,512]{2,0,1:T(8,128)(2,1)} %copy.188), calls=%async_computation.4 | async-start | bytes 786432 | tf_op jit(solution)/shard_map/all_to_all | solution.py:84
  78.6 34.6 %all-to-all-start.1 = ((bf16[48,8,512]{2,0,1:T(8,128)(2,1)}), bf16[48,8,512]{2,0,1:T(8,128)(2,1)}, u32[]{:S(2)}, u32[]{:S(2)}) async-start(bf16[48,8,512]{2,0,1:T(8,128)(2,1)} %copy.182), calls=%async_computation.1 | async-start | bytes 786432 | tf_op jit(solution)/shard_map/all_to_all | solution.py:82
  129.9 56.5 %collective-permute-start.2 = (f32[384,512]{0,1:T(8,128)}, f32[384,512]{0,1:T(8,128)}, u32[]{:S(2)}, u32[]{:S(2)}) collective-permute-start(f32[384,512]{0,1:T(8,128)} %bitcast_add_fusion.4), channel_id=1, source_target_pairs={{0,1},{1,2},{2,3},{3,4},{4,5},{5,6},{6,7},{7,0},{8,9},{9,10},{10,1... | collective-permute-start | bytes 2359304 | tf_op jit(solution)/shard_map/while/body/eval_jaxpr/ppermute | solution.py:18
  131.1 56.2 %copy-start.13 = (s32[1,24]{1,0:T(1,128)S(1)}, s32[1,24]{1,0:T(1,128)}, u32[]{:S(2)}) copy-start(s32[1,24]{1,0:T(1,128)} %get-tuple-element.772) | copy-start | bytes 292 | tf_op jit(solution)/shard_map/while
  131.2 56.2 %copy-start.15 = (s32[1,24]{1,0:T(1,128)S(1)}, s32[1,24]{1,0:T(1,128)}, u32[]{:S(2)}) copy-start(s32[1,24]{1,0:T(1,128)} %get-tuple-element.794) | copy-start | bytes 292 | tf_op jit(solution)/shard_map/while
  131.3 55.2 %collective-permute-start.3 = (f32[384,512]{0,1:T(8,128)S(1)}, f32[384,512]{0,1:T(8,128)S(1)}, u32[]{:S(2)}, u32[]{:S(2)}) collective-permute-start(f32[384,512]{0,1:T(8,128)S(1)} %bitcast_add_fusion.5), channel_id=1, source_target_pairs={{0,1},{1,2},{2,3},{3,4},{4,5},{5,6},{6,7},{7,0},{8,9},{9,10},{10,1... | collective-permute-start | bytes 2359304 | tf_op jit(solution)/shard_map/while/body/eval_jaxpr/ppermute | solution.py:18
  132.0 47.6 %collective-permute-start = (bf16[384,512]{1,0:T(8,128)(2,1)}, bf16[384,512]{1,0:T(8,128)(2,1)}, u32[]{:S(2)}, u32[]{:S(2)}) collective-permute-start(bf16[384,512]{1,0:T(8,128)(2,1)} %copy.260), channel_id=1, source_target_pairs={{0,1},{1,2},{2,3},{3,4},{4,5},{5,6},{6,7},{7,0},{8,9},{9,10},{10,1... | collective-permute-start | bytes 1179656 | tf_op jit(solution)/shard_map/while/body/eval_jaxpr/ppermute | solution.py:18
  134.0 52.4 %collective-permute-start.1 = (bf16[384,512]{1,0:T(8,128)(2,1)}, bf16[384,512]{1,0:T(8,128)(2,1)}, u32[]{:S(2)}, u32[]{:S(2)}) collective-permute-start(bf16[384,512]{1,0:T(8,128)(2,1)} %copy.261), channel_id=1, source_target_pairs={{0,1},{1,2},{2,3},{3,4},{4,5},{5,6},{6,7},{7,0},{8,9},{9,10},{10,1... | collective-permute-start | bytes 1179656 | tf_op jit(solution)/shard_map/while/body/eval_jaxpr/ppermute | solution.py:18
  202.1 55.6 %collective-permute-start.2 = (f32[384,512]{0,1:T(8,128)}, f32[384,512]{0,1:T(8,128)}, u32[]{:S(2)}, u32[]{:S(2)}) collective-permute-start(f32[384,512]{0,1:T(8,128)} %bitcast_add_fusion.4), channel_id=1, source_target_pairs={{0,1},{1,2},{2,3},{3,4},{4,5},{5,6},{6,7},{7,0},{8,9},{9,10},{10,1... | collective-permute-start | bytes 2359304 | tf_op jit(solution)/shard_map/while/body/eval_jaxpr/ppermute | solution.py:18
  203.2 55.4 %copy-start.13 = (s32[1,24]{1,0:T(1,128)S(1)}, s32[1,24]{1,0:T(1,128)}, u32[]{:S(2)}) copy-start(s32[1,24]{1,0:T(1,128)} %get-tuple-element.772) | copy-start | bytes 292 | tf_op jit(solution)/shard_map/while
  203.2 55.4 %copy-start.15 = (s32[1,24]{1,0:T(1,128)S(1)}, s32[1,24]{1,0:T(1,128)}, u32[]{:S(2)}) copy-start(s32[1,24]{1,0:T(1,128)} %get-tuple-element.794) | copy-start | bytes 292 | tf_op jit(solution)/shard_map/while
  203.3 54.4 %collective-permute-start.3 = (f32[384,512]{0,1:T(8,128)S(1)}, f32[384,512]{0,1:T(8,128)S(1)}, u32[]{:S(2)}, u32[]{:S(2)}) collective-permute-start(f32[384,512]{0,1:T(8,128)S(1)} %bitcast_add_fusion.5), channel_id=1, source_target_pairs={{0,1},{1,2},{2,3},{3,4},{4,5},{5,6},{6,7},{7,0},{8,9},{9,10},{10,1... | collective-permute-start | bytes 2359304 | tf_op jit(solution)/shard_map/while/body/eval_jaxpr/ppermute | solution.py:18
  203.4 48.4 %collective-permute-start = (bf16[384,512]{1,0:T(8,128)(2,1)}, bf16[384,512]{1,0:T(8,128)(2,1)}, u32[]{:S(2)}, u32[]{:S(2)}) collective-permute-start(bf16[384,512]{1,0:T(8,128)(2,1)} %copy.260), channel_id=1, source_target_pairs={{0,1},{1,2},{2,3},{3,4},{4,5},{5,6},{6,7},{7,0},{8,9},{9,10},{10,1... | collective-permute-start | bytes 1179656 | tf_op jit(solution)/shard_map/while/body/eval_jaxpr/ppermute | solution.py:18
  203.5 54.2 %collective-permute-start.1 = (bf16[384,512]{1,0:T(8,128)(2,1)}, bf16[384,512]{1,0:T(8,128)(2,1)}, u32[]{:S(2)}, u32[]{:S(2)}) collective-permute-start(bf16[384,512]{1,0:T(8,128)(2,1)} %copy.261), channel_id=1, source_target_pairs={{0,1},{1,2},{2,3},{3,4},{4,5},{5,6},{6,7},{7,0},{8,9},{9,10},{10,1... | collective-permute-start | bytes 1179656 | tf_op jit(solution)/shard_map/while/body/eval_jaxpr/ppermute | solution.py:18
  273.4 54.7 %collective-permute-start.2 = (f32[384,512]{0,1:T(8,128)}, f32[384,512]{0,1:T(8,128)}, u32[]{:S(2)}, u32[]{:S(2)}) collective-permute-start(f32[384,512]{0,1:T(8,128)} %bitcast_add_fusion.4), channel_id=1, source_target_pairs={{0,1},{1,2},{2,3},{3,4},{4,5},{5,6},{6,7},{7,0},{8,9},{9,10},{10,1... | collective-permute-start | bytes 2359304 | tf_op jit(solution)/shard_map/while/body/eval_jaxpr/ppermute | solution.py:18
  274.5 54.4 %copy-start.13 = (s32[1,24]{1,0:T(1,128)S(1)}, s32[1,24]{1,0:T(1,128)}, u32[]{:S(2)}) copy-start(s32[1,24]{1,0:T(1,128)} %get-tuple-element.772) | copy-start | bytes 292 | tf_op jit(solution)/shard_map/while
  274.5 54.4 %copy-start.15 = (s32[1,24]{1,0:T(1,128)S(1)}, s32[1,24]{1,0:T(1,128)}, u32[]{:S(2)}) copy-start(s32[1,24]{1,0:T(1,128)} %get-tuple-element.794) | copy-start | bytes 292 | tf_op jit(solution)/shard_map/while
  274.6 53.5 %collective-permute-start.3 = (f32[384,512]{0,1:T(8,128)S(1)}, f32[384,512]{0,1:T(8,128)S(1)}, u32[]{:S(2)}, u32[]{:S(2)}) collective-permute-start(f32[384,512]{0,1:T(8,128)S(1)} %bitcast_add_fusion.5), channel_id=1, source_target_pairs={{0,1},{1,2},{2,3},{3,4},{4,5},{5,6},{6,7},{7,0},{8,9},{9,10},{10,1... | collective-permute-start | bytes 2359304 | tf_op jit(solution)/shard_map/while/body/eval_jaxpr/ppermute | solution.py:18
  274.7 48.4 %collective-permute-start = (bf16[384,512]{1,0:T(8,128)(2,1)}, bf16[384,512]{1,0:T(8,128)(2,1)}, u32[]{:S(2)}, u32[]{:S(2)}) collective-permute-start(bf16[384,512]{1,0:T(8,128)(2,1)} %copy.260), channel_id=1, source_target_pairs={{0,1},{1,2},{2,3},{3,4},{4,5},{5,6},{6,7},{7,0},{8,9},{9,10},{10,1... | collective-permute-start | bytes 1179656 | tf_op jit(solution)/shard_map/while/body/eval_jaxpr/ppermute | solution.py:18
  274.8 53.3 %collective-permute-start.1 = (bf16[384,512]{1,0:T(8,128)(2,1)}, bf16[384,512]{1,0:T(8,128)(2,1)}, u32[]{:S(2)}, u32[]{:S(2)}) collective-permute-start(bf16[384,512]{1,0:T(8,128)(2,1)} %copy.261), channel_id=1, source_target_pairs={{0,1},{1,2},{2,3},{3,4},{4,5},{5,6},{6,7},{7,0},{8,9},{9,10},{10,1... | collective-permute-start | bytes 1179656 | tf_op jit(solution)/shard_map/while/body/eval_jaxpr/ppermute | solution.py:18
  343.7 53.7 %collective-permute-start.2 = (f32[384,512]{0,1:T(8,128)}, f32[384,512]{0,1:T(8,128)}, u32[]{:S(2)}, u32[]{:S(2)}) collective-permute-start(f32[384,512]{0,1:T(8,128)} %bitcast_add_fusion.4), channel_id=1, source_target_pairs={{0,1},{1,2},{2,3},{3,4},{4,5},{5,6},{6,7},{7,0},{8,9},{9,10},{10,1... | collective-permute-start | bytes 2359304 | tf_op jit(solution)/shard_map/while/body/eval_jaxpr/ppermute | solution.py:18
  344.9 53.5 %copy-start.13 = (s32[1,24]{1,0:T(1,128)S(1)}, s32[1,24]{1,0:T(1,128)}, u32[]{:S(2)}) copy-start(s32[1,24]{1,0:T(1,128)} %get-tuple-element.772) | copy-start | bytes 292 | tf_op jit(solution)/shard_map/while
  344.9 53.5 %copy-start.15 = (s32[1,24]{1,0:T(1,128)S(1)}, s32[1,24]{1,0:T(1,128)}, u32[]{:S(2)}) copy-start(s32[1,24]{1,0:T(1,128)} %get-tuple-element.794) | copy-start | bytes 292 | tf_op jit(solution)/shard_map/while
  344.9 52.5 %collective-permute-start.3 = (f32[384,512]{0,1:T(8,128)S(1)}, f32[384,512]{0,1:T(8,128)S(1)}, u32[]{:S(2)}, u32[]{:S(2)}) collective-permute-start(f32[384,512]{0,1:T(8,128)S(1)} %bitcast_add_fusion.5), channel_id=1, source_target_pairs={{0,1},{1,2},{2,3},{3,4},{4,5},{5,6},{6,7},{7,0},{8,9},{9,10},{10,1... | collective-permute-start | bytes 2359304 | tf_op jit(solution)/shard_map/while/body/eval_jaxpr/ppermute | solution.py:18
  345.0 48.2 %collective-permute-start = (bf16[384,512]{1,0:T(8,128)(2,1)}, bf16[384,512]{1,0:T(8,128)(2,1)}, u32[]{:S(2)}, u32[]{:S(2)}) collective-permute-start(bf16[384,512]{1,0:T(8,128)(2,1)} %copy.260), channel_id=1, source_target_pairs={{0,1},{1,2},{2,3},{3,4},{4,5},{5,6},{6,7},{7,0},{8,9},{9,10},{10,1... | collective-permute-start | bytes 1179656 | tf_op jit(solution)/shard_map/while/body/eval_jaxpr/ppermute | solution.py:18
  345.1 52.3 %collective-permute-start.1 = (bf16[384,512]{1,0:T(8,128)(2,1)}, bf16[384,512]{1,0:T(8,128)(2,1)}, u32[]{:S(2)}, u32[]{:S(2)}) collective-permute-start(bf16[384,512]{1,0:T(8,128)(2,1)} %copy.261), channel_id=1, source_target_pairs={{0,1},{1,2},{2,3},{3,4},{4,5},{5,6},{6,7},{7,0},{8,9},{9,10},{10,1... | collective-permute-start | bytes 1179656 | tf_op jit(solution)/shard_map/while/body/eval_jaxpr/ppermute | solution.py:18
  413.1 52.8 %collective-permute-start.2 = (f32[384,512]{0,1:T(8,128)}, f32[384,512]{0,1:T(8,128)}, u32[]{:S(2)}, u32[]{:S(2)}) collective-permute-start(f32[384,512]{0,1:T(8,128)} %bitcast_add_fusion.4), channel_id=1, source_target_pairs={{0,1},{1,2},{2,3},{3,4},{4,5},{5,6},{6,7},{7,0},{8,9},{9,10},{10,1... | collective-permute-start | bytes 2359304 | tf_op jit(solution)/shard_map/while/body/eval_jaxpr/ppermute | solution.py:18
  414.3 52.6 %copy-start.13 = (s32[1,24]{1,0:T(1,128)S(1)}, s32[1,24]{1,0:T(1,128)}, u32[]{:S(2)}) copy-start(s32[1,24]{1,0:T(1,128)} %get-tuple-element.772) | copy-start | bytes 292 | tf_op jit(solution)/shard_map/while
  414.3 52.6 %copy-start.15 = (s32[1,24]{1,0:T(1,128)S(1)}, s32[1,24]{1,0:T(1,128)}, u32[]{:S(2)}) copy-start(s32[1,24]{1,0:T(1,128)} %get-tuple-element.794) | copy-start | bytes 292 | tf_op jit(solution)/shard_map/while
  414.4 51.6 %collective-permute-start.3 = (f32[384,512]{0,1:T(8,128)S(1)}, f32[384,512]{0,1:T(8,128)S(1)}, u32[]{:S(2)}, u32[]{:S(2)}) collective-permute-start(f32[384,512]{0,1:T(8,128)S(1)} %bitcast_add_fusion.5), channel_id=1, source_target_pairs={{0,1},{1,2},{2,3},{3,4},{4,5},{5,6},{6,7},{7,0},{8,9},{9,10},{10,1... | collective-permute-start | bytes 2359304 | tf_op jit(solution)/shard_map/while/body/eval_jaxpr/ppermute | solution.py:18
  414.5 47.3 %collective-permute-start = (bf16[384,512]{1,0:T(8,128)(2,1)}, bf16[384,512]{1,0:T(8,128)(2,1)}, u32[]{:S(2)}, u32[]{:S(2)}) collective-permute-start(bf16[384,512]{1,0:T(8,128)(2,1)} %copy.260), channel_id=1, source_target_pairs={{0,1},{1,2},{2,3},{3,4},{4,5},{5,6},{6,7},{7,0},{8,9},{9,10},{10,1... | collective-permute-start | bytes 1179656 | tf_op jit(solution)/shard_map/while/body/eval_jaxpr/ppermute | solution.py:18
  414.5 51.4 %collective-permute-start.1 = (bf16[384,512]{1,0:T(8,128)(2,1)}, bf16[384,512]{1,0:T(8,128)(2,1)}, u32[]{:S(2)}, u32[]{:S(2)}) collective-permute-start(bf16[384,512]{1,0:T(8,128)(2,1)} %copy.261), channel_id=1, source_target_pairs={{0,1},{1,2},{2,3},{3,4},{4,5},{5,6},{6,7},{7,0},{8,9},{9,10},{10,1... | collective-permute-start | bytes 1179656 | tf_op jit(solution)/shard_map/while/body/eval_jaxpr/ppermute | solution.py:18
  481.7 51.9 %collective-permute-start.2 = (f32[384,512]{0,1:T(8,128)}, f32[384,512]{0,1:T(8,128)}, u32[]{:S(2)}, u32[]{:S(2)}) collective-permute-start(f32[384,512]{0,1:T(8,128)} %bitcast_add_fusion.4), channel_id=1, source_target_pairs={{0,1},{1,2},{2,3},{3,4},{4,5},{5,6},{6,7},{7,0},{8,9},{9,10},{10,1... | collective-permute-start | bytes 2359304 | tf_op jit(solution)/shard_map/while/body/eval_jaxpr/ppermute | solution.py:18
  482.9 50.7 %collective-permute-start.3 = (f32[384,512]{0,1:T(8,128)S(1)}, f32[384,512]{0,1:T(8,128)S(1)}, u32[]{:S(2)}, u32[]{:S(2)}) collective-permute-start(f32[384,512]{0,1:T(8,128)S(1)} %bitcast_add_fusion.5), channel_id=1, source_target_pairs={{0,1},{1,2},{2,3},{3,4},{4,5},{5,6},{6,7},{7,0},{8,9},{9,10},{10,1... | collective-permute-start | bytes 2359304 | tf_op jit(solution)/shard_map/while/body/eval_jaxpr/ppermute | solution.py:18
  483.0 46.4 %collective-permute-start = (bf16[384,512]{1,0:T(8,128)(2,1)}, bf16[384,512]{1,0:T(8,128)(2,1)}, u32[]{:S(2)}, u32[]{:S(2)}) collective-permute-start(bf16[384,512]{1,0:T(8,128)(2,1)} %copy.260), channel_id=1, source_target_pairs={{0,1},{1,2},{2,3},{3,4},{4,5},{5,6},{6,7},{7,0},{8,9},{9,10},{10,1... | collective-permute-start | bytes 1179656 | tf_op jit(solution)/shard_map/while/body/eval_jaxpr/ppermute | solution.py:18
  483.1 50.5 %collective-permute-start.1 = (bf16[384,512]{1,0:T(8,128)(2,1)}, bf16[384,512]{1,0:T(8,128)(2,1)}, u32[]{:S(2)}, u32[]{:S(2)}) collective-permute-start(bf16[384,512]{1,0:T(8,128)(2,1)} %copy.261), channel_id=1, source_target_pairs={{0,1},{1,2},{2,3},{3,4},{4,5},{5,6},{6,7},{7,0},{8,9},{9,10},{10,1... | collective-permute-start | bytes 1179656 | tf_op jit(solution)/shard_map/while/body/eval_jaxpr/ppermute | solution.py:18
  549.2 51.0 %collective-permute-start.2 = (f32[384,512]{0,1:T(8,128)}, f32[384,512]{0,1:T(8,128)}, u32[]{:S(2)}, u32[]{:S(2)}) collective-permute-start(f32[384,512]{0,1:T(8,128)} %bitcast_add_fusion.4), channel_id=1, source_target_pairs={{0,1},{1,2},{2,3},{3,4},{4,5},{5,6},{6,7},{7,0},{8,9},{9,10},{10,1... | collective-permute-start | bytes 2359304 | tf_op jit(solution)/shard_map/while/body/eval_jaxpr/ppermute | solution.py:18
  550.5 49.8 %collective-permute-start.3 = (f32[384,512]{0,1:T(8,128)S(1)}, f32[384,512]{0,1:T(8,128)S(1)}, u32[]{:S(2)}, u32[]{:S(2)}) collective-permute-start(f32[384,512]{0,1:T(8,128)S(1)} %bitcast_add_fusion.5), channel_id=1, source_target_pairs={{0,1},{1,2},{2,3},{3,4},{4,5},{5,6},{6,7},{7,0},{8,9},{9,10},{10,1... | collective-permute-start | bytes 2359304 | tf_op jit(solution)/shard_map/while/body/eval_jaxpr/ppermute | solution.py:18
  550.5 45.5 %collective-permute-start = (bf16[384,512]{1,0:T(8,128)(2,1)}, bf16[384,512]{1,0:T(8,128)(2,1)}, u32[]{:S(2)}, u32[]{:S(2)}) collective-permute-start(bf16[384,512]{1,0:T(8,128)(2,1)} %copy.260), channel_id=1, source_target_pairs={{0,1},{1,2},{2,3},{3,4},{4,5},{5,6},{6,7},{7,0},{8,9},{9,10},{10,1... | collective-permute-start | bytes 1179656 | tf_op jit(solution)/shard_map/while/body/eval_jaxpr/ppermute | solution.py:18
  550.6 49.6 %collective-permute-start.1 = (bf16[384,512]{1,0:T(8,128)(2,1)}, bf16[384,512]{1,0:T(8,128)(2,1)}, u32[]{:S(2)}, u32[]{:S(2)}) collective-permute-start(bf16[384,512]{1,0:T(8,128)(2,1)} %copy.261), channel_id=1, source_target_pairs={{0,1},{1,2},{2,3},{3,4},{4,5},{5,6},{6,7},{7,0},{8,9},{9,10},{10,1... | collective-permute-start | bytes 1179656 | tf_op jit(solution)/shard_map/while/body/eval_jaxpr/ppermute | solution.py:18
  610.2 24.0 %all-to-all-start.5 = ((bf16[8,48,512]{2,1,0:T(8,128)(2,1)}), bf16[8,48,512]{2,1,0:T(8,128)(2,1)S(1)}, u32[]{:S(2)}, u32[]{:S(2)}) async-start(bf16[8,48,512]{2,1,0:T(8,128)(2,1)} %convert_element_type.59), calls=%async_computation.5 | async-start | bytes 786432 | tf_op jit(solution)/shard_map/all_to_all | solution.py:148
  622.6 11.6 %collective-permute-start.5 = (bf16[384,512]{1,0:T(8,128)(2,1)S(1)}, bf16[384,512]{1,0:T(8,128)(2,1)}, u32[]{:S(2)}, u32[]{:S(2)}) collective-permute-start(bf16[384,512]{1,0:T(8,128)(2,1)S(1)} %add.262), channel_id=1, source_target_pairs={{0,1},{1,2},{2,3},{3,4},{4,5},{5,6},{6,7},{7,0},{8,9},{9,10},{10,1... | collective-permute-start | bytes 1179656 | tf_op jit(solution)/shard_map/ppermute | solution.py:18
  634.2 22.1 %all-to-all-start.7 = ((bf16[8,48,512]{2,1,0:T(8,128)(2,1)}), bf16[8,48,512]{2,1,0:T(8,128)(2,1)}, u32[]{:S(2)}, u32[]{:S(2)}) async-start(bf16[8,48,512]{2,1,0:T(8,128)(2,1)} %bitcast.22), calls=%async_computation.7 | async-start | bytes 786432 | tf_op jit(solution)/shard_map/all_to_all | solution.py:154
  644.8 11.6 %collective-permute-start.4 = (bf16[384,512]{1,0:T(8,128)(2,1)S(1)}, bf16[384,512]{1,0:T(8,128)(2,1)}, u32[]{:S(2)}, u32[]{:S(2)}) collective-permute-start(bf16[384,512]{1,0:T(8,128)(2,1)S(1)} %add.261), channel_id=1, source_target_pairs={{0,1},{1,2},{2,3},{3,4},{4,5},{5,6},{6,7},{7,0},{8,9},{9,10},{10,1... | collective-permute-start | bytes 1179656 | tf_op jit(solution)/shard_map/ppermute | solution.py:18
  656.3 17.6 %all-to-all-start.6 = ((bf16[8,48,512]{2,1,0:T(8,128)(2,1)}), bf16[8,48,512]{2,1,0:T(8,128)(2,1)S(1)}, u32[]{:S(2)}, u32[]{:S(2)}) async-start(bf16[8,48,512]{2,1,0:T(8,128)(2,1)} %bitcast.18), calls=%async_computation.6 | async-start | bytes 786432 | tf_op jit(solution)/shard_map/all_to_all | solution.py:151
  (42 other events, 373.6 us)
Sparse Core Ops, SparseCore 0:
  30.4 65.5 all-gather.1
where the time goes:
time: 686 us; the launch traced here: 682 us
  waiting for transfers between devices  387 us (56%)
  local copies, waits for them, and re-layouts  78.6 us (11%)
  matrix products  77.1 us (11%)
  starting transfers between devices  71.6 us (10%)
  other arithmetic  31.2 us (5%)
  blocking collectives  21.7 us (3%)
  between operations  14.3 us (2%)
    ppermute x30, waiting for transfers between devices, passed_along(): return lax.ppermute(value, axis, pairs)  344 us
    while x98, local copies, waits for them, and re-layouts  35.3 us
    ppermute x30, starting transfers between devices, passed_along(): return lax.ppermute(value, axis, pairs)  29 us
    dot_general x9, matrix products, score_tile(): jnp.einsum('qhd,khd->hqk', query_heads, key_heads, preferred_element_type...  22.4 us
    all_to_all x1, blocking collectives, local(): lax.all_to_all(keys[0], 'head', split_axis=1, concat_axis=0, tiled=True)  21.7 us
    dot_general x8, matrix products, tile_grads(): jnp.einsum('hqk,khd->qhd', score_grad, key_heads, preferred_element_type=...  18.6 us
    dot_general x8, matrix products, tile_grads(): jnp.einsum('hqk,qhd->khd', score_grad, query_heads, preferred_element_typ...  18.5 us
    add x8, other arithmetic, key_visit(): running[1] + pieces[1].reshape(running[1].shape)  16.9 us
  transfers between devices with their start and end apart: 38, of which 21 were waited for; matrix products, arithmetic and copies ran while one was open for 9% of the time, Pallas kernels for 0%

commit v1 on v0

v1 whole, which is shorter than its diff:
```python
import functools
import math

import jax
import jax.numpy as jnp
from jax import lax
from jax.experimental import pallas as pl
from jax.experimental.pallas import tpu as pltpu
from jax.sharding import Mesh, PartitionSpec as P

HD = 128
BLOCK = 128
HEADS = 32
ROWS = 48
CHUNKS = 32
HALF = ROWS * CHUNKS
OWN_BLOCKS = HALF // BLOCK
ALL_BLOCKS = 2 * OWN_BLOCKS
PAD_BLOCKS = ALL_BLOCKS + 4
EXTRA = 16
SCALE = 1.0 / math.sqrt(HD)
SCALE_LOG2 = SCALE * math.log2(math.e)
NEG_FILL = -1e30
WINDOWS = ((2, 1), (4, 3), (8, 5), (12, 9))

CONTRACT_LAST = (((1,), (1,)), ((), ()))


def split_pair_kernel(first_ref, second_ref, out_ref):
    for head in range(HEADS):
        columns = slice(head * HD, (head + 1) * HD)
        out_ref[head, 0] = first_ref[:, columns]
        out_ref[head, 1] = second_ref[:, columns]


def split_pair(first, second):
    return pl.pallas_call(
        split_pair_kernel,
        out_shape=jax.ShapeDtypeStruct((HEADS, 2, ROWS, HD), jnp.bfloat16),
        name="split_pair",
    )(first, second)


def split_query_kernel(shift_ref, query_ref, grad_ref, output_ref, out_ref):
    lane = lax.broadcasted_iota(jnp.int32, (ROWS, HD), 1)
    dots = jnp.zeros((ROWS, HD), jnp.float32)
    for head in range(HEADS):
        columns = slice(head * HD, (head + 1) * HD)
        grad = grad_ref[:, columns]
        out_ref[head, 0:ROWS] = query_ref[:, columns]
        out_ref[head, ROWS : 2 * ROWS] = grad
        dot = jnp.sum(
            grad.astype(jnp.float32) * output_ref[:, columns].astype(jnp.float32),
            axis=1,
            keepdims=True,
        )
        dots = jnp.where(lane == head, dot, dots)
    by_head = jnp.concatenate([dots, jnp.zeros((HD - ROWS, HD), jnp.float32)], axis=0).T
    by_head = pltpu.roll(by_head[:HEADS], shift_ref[0], 1)
    high = by_head.astype(jnp.bfloat16).astype(jnp.float32)
    rest = by_head - high
    middle = rest.astype(jnp.bfloat16).astype(jnp.float32)
    low = rest - middle
    row = lax.broadcasted_iota(jnp.int32, (HEADS, EXTRA, HD), 1)
    parts = jnp.where(row == 0, high[:, None, :], 0.0)
    parts = jnp.where(row == 1, middle[:, None, :], parts)
    parts = jnp.where(row == 2, low[:, None, :], parts)
    out_ref[:, 2 * ROWS :, :] = parts.astype(jnp.bfloat16)


def split_query(shift, query, grad, output):
    return pl.pallas_call(
        split_query_kernel,
        out_shape=jax.ShapeDtypeStruct((HEADS, 2 * ROWS + EXTRA, HD), jnp.bfloat16),
        in_specs=[pl.BlockSpec(memory_space=pltpu.SMEM)]
        + [pl.BlockSpec(memory_space=pltpu.VMEM)] * 3,
        name="split_query",
    )(shift, query, grad, output)


def grads_kernel(
    meta_ref,
    queries_ref,
    own_ref,
    other_ref,
    query_grad_ref,
    own_grad_ref,
    other_grad_ref,
    query_s,
    grad_s,
    dot_s,
    key_s,
    value_s,
    keyt_s,
    key_acc,
    value_acc,
    dq_s,
):
    query_s[...] = queries_ref[:, 0:ROWS].reshape(HALF, HD)
    grad_s[...] = queries_ref[:, ROWS : 2 * ROWS].reshape(HALF, HD)
    parts = queries_ref[:, 2 * ROWS :].astype(jnp.float32)
    dots = parts[:, 0, :] + parts[:, 1, :] + parts[:, 2, :]
    lane = lax.broadcasted_iota(jnp.int32, (1, HD), 1)
    for group in range(4):
        piece = [dots[group * 8 + z : group * 8 + z + 1] for z in range(8)]
        blocks = (
            piece[0] + piece[1] + jnp.where(lane >= 96, piece[2], 0.0),
            jnp.where(lane < 16, piece[2], 0.0)
            + piece[3]
            + piece[4]
            + jnp.where(lane >= 112, piece[5], 0.0),
            jnp.where(lane < 32, piece[5], 0.0) + piece[6] + piece[7],
        )
        for index in range(3):
            dot_s[3 * group + index : 3 * group + index + 1, :] = blocks[index]
    tail = ALL_BLOCKS * BLOCK
    pad = (PAD_BLOCKS - ALL_BLOCKS) * BLOCK
    key_s[tail:, :] = jnp.zeros((pad, HD), jnp.bfloat16)
    value_s[tail:, :] = jnp.zeros((pad, HD), jnp.bfloat16)
    keyt_s[:, tail:] = jnp.zeros((HD, pad), jnp.bfloat16)
    key_acc[...] = jnp.zeros(key_acc.shape, jnp.float32)
    value_acc[...] = jnp.zeros(value_acc.shape, jnp.float32)
    for side, pair_ref in ((0, own_ref), (1, other_ref)):
        keys = pair_ref[:, 0].reshape(HALF, HD)
        values = pair_ref[:, 1].reshape(HALF, HD)
        for block in range(OWN_BLOCKS):
            rows = slice(block * BLOCK, (block + 1) * BLOCK)
            place = pl.multiple_of(meta_ref[0, side * OWN_BLOCKS + block] * BLOCK, BLOCK)
            key_s[pl.ds(place, BLOCK), :] = keys[rows]
            value_s[pl.ds(place, BLOCK), :] = values[rows]
            keyt_s[:, pl.ds(place, BLOCK)] = keys[rows].T

    def visit(block, width, fewest, position, first):
        rows = pl.ds(pl.multiple_of(block * BLOCK, BLOCK), BLOCK)
        span = pl.ds(pl.multiple_of(first * BLOCK, BLOCK), width * BLOCK)
        query = query_s[rows, :]
        grad = grad_s[rows, :]
        dot = dot_s[pl.ds(block, 1), :]
        scores = lax.dot_general(
            key_s[span, :], query, CONTRACT_LAST, preferred_element_type=jnp.float32
        )
        open_rows = (fewest - 1) * BLOCK
        shape = (width * BLOCK - open_rows, BLOCK)
        ahead = (
            lax.broadcasted_iota(jnp.int32, shape, 0)
            - lax.broadcasted_iota(jnp.int32, shape, 1)
            + open_rows
        )
        masked = jnp.where(ahead <= (position - first) * BLOCK, scores[open_rows:], NEG_FILL)
        if open_rows:
            scores = jnp.concatenate([scores[:open_rows], masked], axis=0)
        else:
            scores = masked
        highest = jnp.max(scores, axis=0, keepdims=True)
        weights = jnp.exp2((scores - highest) * SCALE_LOG2)
        weights = weights * (1.0 / jnp.sum(weights, axis=0, keepdims=True))
        value_acc[span, :] += jnp.dot(
            weights.astype(jnp.bfloat16), grad, preferred_element_type=jnp.float32
        )
        weight_grad = lax.dot_general(
            value_s[span, :], grad, CONTRACT_LAST, preferred_element_type=jnp.float32
        )
        score_grad = (weights * (weight_grad - dot)).astype(jnp.bfloat16)
        key_acc[span, :] += jnp.dot(score_grad, query, preferred_element_type=jnp.float32)
        turned = jnp.dot(keyt_s[:, span], score_grad, preferred_element_type=jnp.float32)
        dq_s[rows, :] = (turned.T * SCALE).astype(jnp.bfloat16)

    def step(block, carry):
        position = meta_ref[0, block]
        first = meta_ref[1, block]
        count = position - first + 1
        most = 0
        for width, fewest in WINDOWS:

            @pl.when((count > most) & (count <= width))
            def _(width=width, fewest=fewest):
                visit(block, width, fewest, position, first)

            most = width
        return carry

    lax.fori_loop(0, OWN_BLOCKS, step, 0)
    query_grad_ref[...] = dq_s[...].reshape(CHUNKS, ROWS, HD)
    for side, out_ref in ((0, own_grad_ref), (1, other_grad_ref)):
        for index, acc, factor in ((0, key_acc, SCALE), (1, value_acc, 1.0)):
            pieces = []
            for block in range(OWN_BLOCKS):
                place = pl.multiple_of(meta_ref[0, side * OWN_BLOCKS + block] * BLOCK, BLOCK)
                pieces.append((acc[pl.ds(place, BLOCK), :] * factor).astype(out_ref.dtype))
            out_ref[:, index] = jnp.concatenate(pieces, axis=0).reshape(CHUNKS, ROWS, HD)


def grads(meta, queries, own, other):
    pair_shape = (CHUNKS, 2, ROWS, HD)
    return pl.pallas_call(
        grads_kernel,
        out_shape=(
            jax.ShapeDtypeStruct((CHUNKS, ROWS, HD), jnp.bfloat16),
            jax.ShapeDtypeStruct(pair_shape, jnp.float32),
            jax.ShapeDtypeStruct(pair_shape, jnp.bfloat16),
        ),
        in_specs=[pl.BlockSpec(memory_space=pltpu.SMEM)]
        + [pl.BlockSpec(memory_space=pltpu.VMEM)] * 3,
        out_specs=[pl.BlockSpec(memory_space=pltpu.VMEM)] * 3,
        scratch_shapes=[
            pltpu.VMEM((HALF, HD), jnp.bfloat16),
            pltpu.VMEM((HALF, HD), jnp.bfloat16),
            pltpu.VMEM((16, HD), jnp.float32),
            pltpu.VMEM((PAD_BLOCKS * BLOCK, HD), jnp.bfloat16),
            pltpu.VMEM((PAD_BLOCKS * BLOCK, HD), jnp.bfloat16),
            pltpu.VMEM((HD, PAD_BLOCKS * BLOCK), jnp.bfloat16),
            pltpu.VMEM((PAD_BLOCKS * BLOCK, HD), jnp.float32),
            pltpu.VMEM((PAD_BLOCKS * BLOCK, HD), jnp.float32),
            pltpu.VMEM((HALF, HD), jnp.bfloat16),
        ],
        compiler_params=pltpu.CompilerParams(vmem_limit_bytes=40 * 1024 * 1024),
        name="grads",
    )(meta, queries, own, other)


def spread(value):
    return lax.all_to_all(value, ("x", "z"), 0, 0, tiled=True)


def swap(value):
    return lax.ppermute(value, "y", [(0, 1), (1, 0)])


def local(queries, keys, values, out_grad, outputs, doc_ids, block_order):
    side = lax.axis_index("y")
    order = block_order[0]
    documents = doc_ids[0]
    starts = jnp.sum((documents[None, :] < documents[:, None]).astype(jnp.int32), axis=1)
    own_first = jnp.where(
        side == 0, order, jnp.concatenate([order[OWN_BLOCKS:], order[:OWN_BLOCKS]])
    )
    table = lax.iota(jnp.int32, ALL_BLOCKS)
    first = jnp.sum(
        jnp.where(own_first[:, None] == table[None, :], starts[None, :], 0), axis=1
    )
    meta = jnp.stack([own_first, first])
    shift = jnp.reshape((lax.axis_index("z") * ROWS) % BLOCK, (1,)).astype(jnp.int32)

    own_pair = spread(split_pair(keys[0], values[0]))
    query_parts = spread(split_query(shift, queries[0], out_grad[0], outputs[0]))
    other_pair = swap(own_pair)
    query_grad, own_grad, other_grad = grads(meta, query_parts, own_pair, other_pair)
    arrived = swap(other_grad)
    query_back = spread(query_grad)
    pair_grad = (own_grad + arrived.astype(jnp.float32)).astype(jnp.bfloat16)
    pair_back = spread(pair_grad)

    def to_rows(by_head):
        return by_head.transpose(1, 0, 2).reshape(1, ROWS, HEADS * HD)

    return (to_rows(query_back), to_rows(pair_back[:, 0]), to_rows(pair_back[:, 1]))


def solution(mesh):
    grid = Mesh(mesh.devices.reshape(8, 4, 2, 4), ("z", "outer", "y", "x"))
    rows = P("outer", ("y", "x", "z"), None)
    whole = P("outer", None)
    return jax.shard_map(
        local,
        mesh=grid,
        in_specs=(rows, rows, rows, rows, rows, whole, whole),
        out_specs=(rows, rows, rows),
        check_vma=False,
    )
```

time: 686 us -> 137 us (0.20)
  waiting for transfers between devices: 387 us -> 76.6 us
  matrix products: 77.1 us -> 0 us
  local copies, waits for them, and re-layouts: 78.6 us -> 5.95 us
  starting transfers between devices: 71.6 us -> 32.1 us
  other arithmetic: 31.2 us -> 1.6 us
  blocking collectives: 21.7 us -> 0 us
  Pallas kernels: 0 us -> 18.2 us
  between operations: 14.3 us -> 0.74 us
    ppermute x30 -> x2, waiting for transfers between devices: 344 us -> 10.2 us  [swap(): return lax.ppermute(value, 'y', [(0, 1), (1, 0)])]
    dot_general x41 -> x0, matrix products: 77.1 us -> none  [the longest x9 22.4 us: score_tile(): jnp.einsum('qhd,khd->hqk', query_heads, key_heads, preferred_element_type...]
    while x101 -> x0, local copies, waits for them, and re-layouts: 38.4 us -> none
    all_to_all x7 -> x4, waiting for transfers between devices: 32.2 us -> 66.5 us  [spread(): return lax.all_to_all(value, ('x', 'z'), 0, 0, tiled=True)]
    ppermute x30 -> x2, starting transfers between devices: 29 us -> 6.26 us  [swap(): return lax.ppermute(value, 'y', [(0, 1), (1, 0)])]
    all_to_all x1 -> x0, blocking collectives: 21.7 us -> none  [local(): lax.all_to_all(keys[0], 'head', split_axis=1, concat_axis=0, tiled=True)]
    add x27 -> x0, other arithmetic: 19.4 us -> none  [the longest x8 16.9 us: key_visit(): running[1] + pieces[1].reshape(running[1].shape)]
    pallas_call x0 -> x3, Pallas kernels: none -> 18.2 us  [the longest x1 13.3 us: grads(): pl.pallas_call(grads_kernel, out_shape=(jax.ShapeDtypeStruct((CHUNKS, ROW...]
  transfers between devices with their start and end apart: 38 -> 6, of which waited for: 21 -> 5; matrix products, arithmetic and copies ran while one was open for 9% -> 2% of each run, Pallas kernels for 0% -> 2%
where the time goes in v1:
time: 137 us; the launch traced here: 135 us
  waiting for transfers between devices  76.6 us (56%)
  starting transfers between devices  32.1 us (23%)
  Pallas kernels  18.2 us (13%)
  local copies, waits for them, and re-layouts  5.95 us (4%)
  other arithmetic  1.6 us (1%)
    all_to_all x4, waiting for transfers between devices, spread(): return lax.all_to_all(value, ('x', 'z'), 0, 0, tiled=True)  66.5 us
    all_to_all x4, starting transfers between devices, spread(): return lax.all_to_all(value, ('x', 'z'), 0, 0, tiled=True)  25.8 us
    pallas_call x1, Pallas kernels, grads(): pl.pallas_call(grads_kernel, out_shape=(jax.ShapeDtypeStruct((CHUNKS, ROW...  13.3 us
    ppermute x2, waiting for transfers between devices, swap(): return lax.ppermute(value, 'y', [(0, 1), (1, 0)])  10.2 us
    ppermute x2, starting transfers between devices, swap(): return lax.ppermute(value, 'y', [(0, 1), (1, 0)])  6.26 us
    unnamed x10, local copies, waits for them, and re-layouts  2.78 us
    reshape x3, local copies, waits for them, and re-layouts, to_rows(): return by_head.transpose(1, 0, 2).reshape(1, ROWS, HEADS * HD)  2.74 us
  transfers between devices with their start and end apart: 6, of which 5 were waited for; matrix products, arithmetic and copies ran while one was open for 2% of the time, Pallas kernels for 2%

profile of v1, /device:TPU:32, one launch (start us, length us, event | category | flops | bytes accessed | tf_op | source)
XLA Modules:
  0.0 135.2 jit_solution(16619210081915897862)
XLA Ops:
  0.6 2.2 %split_pair.1 = bf16[32,2,48,128]{3,2,1,0:T(8,128)(2,1)} custom-call(bf16[48,4096]{1,0:T(8,128)(2,1)} %bitcast.27, bf16[48,4096]{1,0:T(8,128)(2,1)} %bitcast.28), custom_call_target="tpu_custom_call" | custom-call | tf_op jit(solution)/shard_map/split_pair/pallas_call | solution.py:37
  2.8 11.2 %all-to-all-start.1 = ((bf16[32,2,48,128]{3,2,1,0:T(8,128)(2,1)}), bf16[32,2,48,128]{3,2,1,0:T(8,128)(2,1)S(1)}, u32[]{:S(2)}, u32[]{:S(2)}) async-start(bf16[32,2,48,128]{3,2,1,0:T(8,128)(2,1)} %split_pair.1), calls=%async_computation.1 | async-start | bytes 1572864 | tf_op jit(solution)/shard_map/all_to_all | solution.py:222
  14.0 0.0 copy-start.3
  14.0 0.0 copy-start.4
  14.0 2.6 %split_query.1 = bf16[32,112,128]{2,1,0:T(8,128)(2,1)} custom-call(s32[1]{0:T(128)} %bitcast.5.shift_ref, bf16[48,4096]{1,0:T(8,128)(2,1)} %bitcast.24, bf16[48,4096]{1,0:T(8,128)(2,1)} %bitcast.25, bf16[48,4096]{1,0:T(8,128)(2,1)} %bitcast.26), custom_call_target="tpu_custom_call" | custom-call | tf_op jit(solution)/shard_map/split_query/pallas_call | solution.py:72
  16.7 20.5 %all-to-all-done.1.own_ref = bf16[32,2,48,128]{3,2,1,0:T(8,128)(2,1)S(1)} async-done(((bf16[32,2,48,128]{3,2,1,0:T(8,128)(2,1)}), bf16[32,2,48,128]{3,2,1,0:T(8,128)(2,1)S(1)}, u32[]{:S(2)}, u32[]{:S(2)}) %all-to-all-start.1) | async-done | bytes 786464 | tf_op jit(solution)/shard_map/all_to_all | solution.py:222
  37.2 4.9 %all-to-all-start = ((bf16[32,112,128]{2,1,0:T(8,128)(2,1)}), bf16[32,112,128]{2,1,0:T(8,128)(2,1)S(1)}, u32[]{:S(2)}, u32[]{:S(2)}) async-start(bf16[32,112,128]{2,1,0:T(8,128)(2,1)} %split_query.1), calls=%async_computation | async-start | bytes 1835008 | tf_op jit(solution)/shard_map/all_to_all | solution.py:222
  42.1 0.0 copy-done.3
  42.1 0.1 fusion
  42.2 3.2 %collective-permute-start = (bf16[32,2,48,128]{3,2,1,0:T(8,128)(2,1)S(1)}, bf16[32,2,48,128]{3,2,1,0:T(8,128)(2,1)S(1)}, u32[]{:S(2)}, u32[]{:S(2)}) collective-permute-start(bf16[32,2,48,128]{3,2,1,0:T(8,128)(2,1)S(1)} %all-to-all-done.1.own_ref), channel_id=1, source_target_pairs={{0,4},{4,0},{1,5},{5,1},{2,6},{6,2},{3,7},{7,3},{8,12},{12,8},{9,1... | collective-permute-start | bytes 2359304 | tf_op jit(solution)/shard_map/ppermute | solution.py:226
  45.4 0.0 copy-done.4
  45.4 0.2 convert_reduce_fusion
  45.6 0.1 broadcast_select_fusion
  45.7 0.2 select_reduce_fusion
  45.9 0.1 broadcast_select_fusion.1
  45.9 21.5 %all-to-all-done.queries_ref = bf16[32,112,128]{2,1,0:T(8,128)(2,1)S(1)} async-done(((bf16[32,112,128]{2,1,0:T(8,128)(2,1)}), bf16[32,112,128]{2,1,0:T(8,128)(2,1)S(1)}, u32[]{:S(2)}, u32[]{:S(2)}) %all-to-all-start) | async-done | bytes 917536 | tf_op jit(solution)/shard_map/all_to_all | solution.py:222
  67.5 0.0 collective-permute-done.other_ref
  67.5 0.0 copy-start
  67.5 0.9 copy-done
  68.4 0.0 copy-start.1
  68.4 1.1 copy-done.1
  69.5 13.3 %grads.1 = (bf16[32,48,128]{2,1,0:T(8,128)(2,1)S(1)}, f32[32,2,48,128]{3,2,1,0:T(8,128)S(1)}, bf16[32,2,48,128]{3,2,1,0:T(8,128)(2,1)}) custom-call(s32[2,24]{1,0:T(2,128)S(1)} %pad_add_fusion.meta_ref, bf16[32,112,128]{2,1,0:T(8,128)(2,1)S(1)} %all-to-all-done.queries_ref, bf16[32,2,48,128]{3,2,1,0:T(8,128)(2,1)S(1)} %all-to-all-done.1.own_ref, ...), custom_call_target="tpu_custom_call" | custom-call | tf_op jit(solution)/shard_map/grads/pallas_call | solution.py:195
  82.8 0.0 copy-start.2
  82.8 0.7 copy-done.2
  83.6 3.0 %collective-permute-start.1 = (bf16[32,2,48,128]{3,2,1,0:T(8,128)(2,1)}, bf16[32,2,48,128]{3,2,1,0:T(8,128)(2,1)S(1)}, u32[]{:S(2)}, u32[]{:S(2)}) collective-permute-start(bf16[32,2,48,128]{3,2,1,0:T(8,128)(2,1)} %get-tuple-element.8), channel_id=1, source_target_pairs={{0,4},{4,0},{1,5},{5,1},{2,6},{6,2},{3,7},{7,3},{8,12},{12,8},{9,1... | collective-permute-start | bytes 2359304 | tf_op jit(solution)/shard_map/ppermute | solution.py:226
  86.6 5.1 %all-to-all-start.2 = ((bf16[32,48,128]{2,1,0:T(8,128)(2,1)}), bf16[32,48,128]{2,1,0:T(8,128)(2,1)S(1)}, u32[]{:S(2)}, u32[]{:S(2)}) async-start(bf16[32,48,128]{2,1,0:T(8,128)(2,1)} %copy-done.2), calls=%async_computation.2 | async-start | bytes 786432 | tf_op jit(solution)/shard_map/all_to_all | solution.py:222
  91.7 10.2 %collective-permute-done.1 = bf16[32,2,48,128]{3,2,1,0:T(8,128)(2,1)S(1)} collective-permute-done((bf16[32,2,48,128]{3,2,1,0:T(8,128)(2,1)}, bf16[32,2,48,128]{3,2,1,0:T(8,128)(2,1)S(1)}, u32[]{:S(2)}, u32[]{:S(2)}) %collective-permute-start.1) | collective-permute-done | bytes 786464 | tf_op jit(solution)/shard_map/ppermute | solution.py:226
  101.9 1.1 add_convert_fusion
  103.0 2.8 %all-to-all-done.2 = bf16[32,48,128]{2,1,0:T(8,128)(2,1)S(1)} async-done(((bf16[32,48,128]{2,1,0:T(8,128)(2,1)}), bf16[32,48,128]{2,1,0:T(8,128)(2,1)S(1)}, u32[]{:S(2)}, u32[]{:S(2)}) %all-to-all-start.2) | async-done | bytes 393248 | tf_op jit(solution)/shard_map/all_to_all | solution.py:222
  105.7 4.6 %all-to-all-start.3 = ((bf16[32,2,48,128]{3,2,1,0:T(8,128)(2,1)}), bf16[32,2,48,128]{3,2,1,0:T(8,128)(2,1)S(1)}, u32[]{:S(2)}, u32[]{:S(2)}) async-start(bf16[32,2,48,128]{3,2,1,0:T(8,128)(2,1)} %add_convert_fusion), calls=%async_computation.3 | async-start | bytes 1572864 | tf_op jit(solution)/shard_map/all_to_all | solution.py:222
  110.4 0.1 copy.13
  110.5 0.9 reshape.48
  111.4 21.7 %all-to-all-done.3 = bf16[32,2,48,128]{3,2,1,0:T(8,128)(2,1)S(1)} async-done(((bf16[32,2,48,128]{3,2,1,0:T(8,128)(2,1)}), bf16[32,2,48,128]{3,2,1,0:T(8,128)(2,1)S(1)}, u32[]{:S(2)}, u32[]{:S(2)}) %all-to-all-start.3) | async-done | bytes 786464 | tf_op jit(solution)/shard_map/all_to_all | solution.py:222
  133.1 0.1 slice_bitcast_fusion
  133.1 0.1 copy.15
  133.2 0.9 reshape.50
  134.2 0.1 copy.14
  134.3 0.9 reshape.49
  (1 shorter events, 0.0 us)
Async XLA Ops:
  2.8 34.4 %all-to-all-start.1 = ((bf16[32,2,48,128]{3,2,1,0:T(8,128)(2,1)}), bf16[32,2,48,128]{3,2,1,0:T(8,128)(2,1)S(1)}, u32[]{:S(2)}, u32[]{:S(2)}) async-start(bf16[32,2,48,128]{3,2,1,0:T(8,128)(2,1)} %split_pair.1), calls=%async_computation.1 | async-start | bytes 1572864 | tf_op jit(solution)/shard_map/all_to_all | solution.py:222
  14.0 28.1 %copy-start.3 = (s32[1,24]{1,0:T(1,128)S(1)}, s32[1,24]{1,0:T(1,128)}, u32[]{:S(2)}) copy-start(s32[1,24]{1,0:T(1,128)} %param.13) | copy-start | bytes 292
  14.0 31.4 %copy-start.4 = (s32[1,24]{1,0:T(1,128)S(1)}, s32[1,24]{1,0:T(1,128)}, u32[]{:S(2)}) copy-start(s32[1,24]{1,0:T(1,128)} %param.12) | copy-start | bytes 292
  37.2 30.3 %all-to-all-start = ((bf16[32,112,128]{2,1,0:T(8,128)(2,1)}), bf16[32,112,128]{2,1,0:T(8,128)(2,1)S(1)}, u32[]{:S(2)}, u32[]{:S(2)}) async-start(bf16[32,112,128]{2,1,0:T(8,128)(2,1)} %split_query.1), calls=%async_computation | async-start | bytes 1835008 | tf_op jit(solution)/shard_map/all_to_all | solution.py:222
  42.2 25.3 %collective-permute-start = (bf16[32,2,48,128]{3,2,1,0:T(8,128)(2,1)S(1)}, bf16[32,2,48,128]{3,2,1,0:T(8,128)(2,1)S(1)}, u32[]{:S(2)}, u32[]{:S(2)}) collective-permute-start(bf16[32,2,48,128]{3,2,1,0:T(8,128)(2,1)S(1)} %all-to-all-done.1.own_ref), channel_id=1, source_target_pairs={{0,4},{4,0},{1,5},{5,1},{2,6},{6,2},{3,7},{7,3},{8,12},{12,8},{9,1... | collective-permute-start | bytes 2359304 | tf_op jit(solution)/shard_map/ppermute | solution.py:226
  67.5 0.9 copy-start
  68.4 1.1 copy-start.1
  82.8 0.7 copy-start.2
  83.6 18.3 %collective-permute-start.1 = (bf16[32,2,48,128]{3,2,1,0:T(8,128)(2,1)}, bf16[32,2,48,128]{3,2,1,0:T(8,128)(2,1)S(1)}, u32[]{:S(2)}, u32[]{:S(2)}) collective-permute-start(bf16[32,2,48,128]{3,2,1,0:T(8,128)(2,1)} %get-tuple-element.8), channel_id=1, source_target_pairs={{0,4},{4,0},{1,5},{5,1},{2,6},{6,2},{3,7},{7,3},{8,12},{12,8},{9,1... | collective-permute-start | bytes 2359304 | tf_op jit(solution)/shard_map/ppermute | solution.py:226
  86.6 19.1 %all-to-all-start.2 = ((bf16[32,48,128]{2,1,0:T(8,128)(2,1)}), bf16[32,48,128]{2,1,0:T(8,128)(2,1)S(1)}, u32[]{:S(2)}, u32[]{:S(2)}) async-start(bf16[32,48,128]{2,1,0:T(8,128)(2,1)} %copy-done.2), calls=%async_computation.2 | async-start | bytes 786432 | tf_op jit(solution)/shard_map/all_to_all | solution.py:222
  105.7 27.3 %all-to-all-start.3 = ((bf16[32,2,48,128]{3,2,1,0:T(8,128)(2,1)}), bf16[32,2,48,128]{3,2,1,0:T(8,128)(2,1)S(1)}, u32[]{:S(2)}, u32[]{:S(2)}) async-start(bf16[32,2,48,128]{3,2,1,0:T(8,128)(2,1)} %add_convert_fusion), calls=%async_computation.3 | async-start | bytes 1572864 | tf_op jit(solution)/shard_map/all_to_all | solution.py:222

commit v2 on v1

v2 whole, which is shorter than its diff:
```python
import functools
import math

import jax
import jax.numpy as jnp
from jax import lax
from jax.experimental import pallas as pl
from jax.experimental.pallas import tpu as pltpu
from jax.sharding import Mesh, PartitionSpec as P

HD = 128
BLOCK = 128
HEADS = 32
ROWS = 48
CHUNKS = 32
HALF = ROWS * CHUNKS
OWN_BLOCKS = HALF // BLOCK
ALL_BLOCKS = 2 * OWN_BLOCKS
PAD_BLOCKS = ALL_BLOCKS + OWN_BLOCKS
EXTRA = 8
STAT_ROWS = 16
PAD_ROWS = (PAD_BLOCKS - ALL_BLOCKS) * BLOCK
SCALE = 1.0 / math.sqrt(HD)
SCALE_LOG2 = SCALE * math.log2(math.e)
NEG_FILL = -1e30
GROUP = 4
WINDOWS = (2, 4, 8, 12)

CORE0_GROUPS, CORE0_READY = (("k", "v"), ("q", "g")), True
CORE1_GROUPS, CORE1_READY = (("k", "v"), ("q", "g")), False

CONTRACT_LAST = (((1,), (1,)), ((), ()))


def dots_to_rows(shift_ref, dots, out_ref, first_row):
    by_head = jnp.concatenate([dots, jnp.zeros((HD - ROWS, HD), jnp.float32)], axis=0).T
    by_head = pltpu.roll(by_head[:HEADS], shift_ref[0], 1)
    high = by_head.astype(jnp.bfloat16).astype(jnp.float32)
    rest = by_head - high
    middle = rest.astype(jnp.bfloat16).astype(jnp.float32)
    low = rest - middle
    row = lax.broadcasted_iota(jnp.int32, (HEADS, EXTRA, HD), 1)
    parts = jnp.where(row == 0, high[:, None, :], 0.0)
    parts = jnp.where(row == 1, middle[:, None, :], parts)
    parts = jnp.where(row == 2, low[:, None, :], parts)
    out_ref[:, first_row:, :] = parts.astype(jnp.bfloat16)


def pack_kernel(with_dots, shift_ref, *refs):
    out_ref = refs[-1]
    copied = refs[:-2] if with_dots else refs[:-1]
    lane = lax.broadcasted_iota(jnp.int32, (ROWS, HD), 1)
    dots = jnp.zeros((ROWS, HD), jnp.float32)
    for head in range(HEADS):
        columns = slice(head * HD, (head + 1) * HD)
        for index, ref in enumerate(copied):
            out_ref[head, index * ROWS : (index + 1) * ROWS] = ref[:, columns]
        if with_dots:
            dot = jnp.sum(
                copied[-1][:, columns].astype(jnp.float32)
                * refs[-2][:, columns].astype(jnp.float32),
                axis=1,
                keepdims=True,
            )
            dots = jnp.where(lane == head, dot, dots)
    if with_dots:
        dots_to_rows(shift_ref, dots, out_ref, len(copied) * ROWS)


def pack(shift, arrays, outputs=None):
    with_dots = outputs is not None
    operands = [*arrays, outputs] if with_dots else [*arrays]
    rows = len(arrays) * ROWS + (EXTRA if with_dots else 0)
    return pl.pallas_call(
        functools.partial(pack_kernel, with_dots),
        out_shape=jax.ShapeDtypeStruct((HEADS, rows, HD), jnp.bfloat16),
        in_specs=[pl.BlockSpec(memory_space=pltpu.SMEM)]
        + [pl.BlockSpec(memory_space=pltpu.VMEM)] * len(operands),
        name="pack",
    )(shift, *operands)


def grads_kernel(groups, meta_ref, *refs):
    count = len(groups) + 1
    loaded_hbm, refs = refs[:count], refs[count:]
    (query_grad_hbm, own_grad_hbm, other_grad_hbm), refs = refs[:3], refs[3:]
    loaded, refs = refs[:count], refs[count:]
    query_grad_ref, own_grad_ref, other_grad_ref, *refs = refs
    query_s, grad_s, dot_s, key_s, value_s, keyt_s, key_acc, value_acc, dq_s, sem = refs
    loads = [
        pltpu.make_async_copy(source, target, sem.at[index])
        for index, (source, target) in enumerate(zip(loaded_hbm, loaded))
    ]
    for load in loads:
        load.start()
    rows_of = {}
    for ref, names in zip(loaded, (*groups, ("other_k", "other_v"))):
        for index, name in enumerate(names):
            rows_of[name] = ref, index * ROWS

    def rows(name):
        ref, first = rows_of[name]
        return ref[:, first : first + ROWS].reshape(HALF, HD)

    tail = ALL_BLOCKS * BLOCK
    key_s[tail:, :] = jnp.zeros((PAD_ROWS, HD), jnp.bfloat16)
    value_s[tail:, :] = jnp.zeros((PAD_ROWS, HD), jnp.bfloat16)
    keyt_s[:, tail:] = jnp.zeros((HD, PAD_ROWS), jnp.bfloat16)
    key_acc[...] = jnp.zeros(key_acc.shape, jnp.float32)
    value_acc[...] = jnp.zeros(value_acc.shape, jnp.float32)
    for load in loads:
        load.wait()
    for side, names in ((0, ("k", "v")), (1, ("other_k", "other_v"))):
        keys, values = rows(names[0]), rows(names[1])
        for block in range(OWN_BLOCKS):
            stored = slice(block * BLOCK, (block + 1) * BLOCK)
            place = pl.multiple_of(meta_ref[0, side * OWN_BLOCKS + block] * BLOCK, BLOCK)
            key_s[pl.ds(place, BLOCK), :] = keys[stored]
            value_s[pl.ds(place, BLOCK), :] = values[stored]
            keyt_s[:, pl.ds(place, BLOCK)] = keys[stored].T
    query_s[...] = rows("q")
    grad_s[...] = rows("g")
    last, first = rows_of["g"]
    parts = last[:, first + ROWS :].astype(jnp.float32)
    dots = parts[:, 0, :] + parts[:, 1, :] + parts[:, 2, :]
    lane = lax.broadcasted_iota(jnp.int32, (1, HD), 1)
    for group in range(4):
        piece = [dots[group * 8 + z : group * 8 + z + 1] for z in range(8)]
        blocks = (
            piece[0] + piece[1] + jnp.where(lane >= 96, piece[2], 0.0),
            jnp.where(lane < 16, piece[2], 0.0)
            + piece[3]
            + piece[4]
            + jnp.where(lane >= 112, piece[5], 0.0),
            jnp.where(lane < 32, piece[5], 0.0) + piece[6] + piece[7],
        )
        for index in range(3):
            dot_s[3 * group + index : 3 * group + index + 1, :] = blocks[index]

    def visit(blocks, width):
        shape = (width * BLOCK, BLOCK)
        ahead = lax.broadcasted_iota(jnp.int32, shape, 0) - lax.broadcasted_iota(
            jnp.int32, shape, 1
        )
        places, scores, weight_grads = [], [], []
        for block in blocks:
            first = meta_ref[1, block]
            rows = pl.ds(pl.multiple_of(block * BLOCK, BLOCK), BLOCK)
            span = pl.ds(pl.multiple_of(first * BLOCK, BLOCK), width * BLOCK)
            places.append((block, rows, span))
            score = lax.dot_general(
                key_s[span, :],
                query_s[rows, :],
                CONTRACT_LAST,
                preferred_element_type=jnp.float32,
            )
            reach = (meta_ref[0, block] - first) * BLOCK
            scores.append(jnp.where(ahead <= reach, score, NEG_FILL))
            weight_grads.append(
                lax.dot_general(
                    value_s[span, :],
                    grad_s[rows, :],
                    CONTRACT_LAST,
                    preferred_element_type=jnp.float32,
                )
                - dot_s[pl.ds(block, 1), :]
            )
        lows, score_grads = [], []
        for score, weight_grad in zip(scores, weight_grads):
            highest = jnp.max(score, axis=0, keepdims=True)
            weights = jnp.exp2((score - highest) * SCALE_LOG2)
            weights = weights * (1.0 / jnp.sum(weights, axis=0, keepdims=True))
            lows.append(weights.astype(jnp.bfloat16))
            score_grads.append((weights * weight_grad).astype(jnp.bfloat16))
        value_parts, key_parts = [], []
        for (_, rows, span), low, score_grad in zip(places, lows, score_grads):
            value_parts.append(jnp.dot(low, grad_s[rows, :], preferred_element_type=jnp.float32))
            key_parts.append(
                jnp.dot(score_grad, query_s[rows, :], preferred_element_type=jnp.float32)
            )
            turned = jnp.dot(keyt_s[:, span], score_grad, preferred_element_type=jnp.float32)
            dq_s[rows, :] = (turned.T * SCALE).astype(jnp.bfloat16)
        for (_, _, span), value_part, key_part in zip(places, value_parts, key_parts):
            value_acc[span, :] += value_part
            key_acc[span, :] += key_part

    def step(group, carry):
        blocks = [meta_ref[2, group * GROUP + member] for member in range(GROUP)]
        count = meta_ref[0, blocks[0]] - meta_ref[1, blocks[0]] + 1
        most = 0
        for width in WINDOWS:

            @pl.when((count > most) & (count <= width))
            def _(width=width):
                visit(blocks, width)

            most = width
        return carry

    lax.fori_loop(0, OWN_BLOCKS // GROUP, step, 0)
    stores = [
        pltpu.make_async_copy(source, target, sem.at[count + index])
        for index, (source, target) in enumerate(
            (
                (query_grad_ref, query_grad_hbm),
                (other_grad_ref, other_grad_hbm),
                (own_grad_ref, own_grad_hbm),
            )
        )
    ]
    query_grad_ref[...] = dq_s[...].reshape(CHUNKS, ROWS, HD)
    stores[0].start()
    for side, out_ref in ((1, other_grad_ref), (0, own_grad_ref)):
        for index, acc, factor in ((0, key_acc, SCALE), (1, value_acc, 1.0)):
            pieces = []
            for block in range(OWN_BLOCKS):
                place = pl.multiple_of(meta_ref[0, side * OWN_BLOCKS + block] * BLOCK, BLOCK)
                pieces.append((acc[pl.ds(place, BLOCK), :] * factor).astype(out_ref.dtype))
            out_ref[:, index * ROWS : (index + 1) * ROWS] = jnp.concatenate(
                pieces, axis=0
            ).reshape(CHUNKS, ROWS, HD)
        stores[2 - side].start()
    for store in stores:
        store.wait()


def grads(groups, meta, arrays, other):
    pair_shape = (CHUNKS, 2 * ROWS, HD)
    return pl.pallas_call(
        functools.partial(grads_kernel, groups),
        out_shape=(
            pltpu.HBM((CHUNKS, ROWS, HD), jnp.bfloat16),
            jax.ShapeDtypeStruct(pair_shape, jnp.float32),
            pltpu.HBM(pair_shape, jnp.bfloat16),
        ),
        in_specs=[pl.BlockSpec(memory_space=pltpu.SMEM)]
        + [pl.BlockSpec(memory_space=pl.ANY)] * (len(arrays) + 1),
        out_specs=[pl.BlockSpec(memory_space=pl.ANY)] * 3,
        scratch_shapes=[pltpu.VMEM(array.shape, jnp.bfloat16) for array in (*arrays, other)]
        + [
            pltpu.VMEM((CHUNKS, ROWS, HD), jnp.bfloat16),
            pltpu.VMEM(pair_shape, jnp.float32),
            pltpu.VMEM(pair_shape, jnp.bfloat16),
            pltpu.VMEM((HALF, HD), jnp.bfloat16),
            pltpu.VMEM((HALF, HD), jnp.bfloat16),
            pltpu.VMEM((STAT_ROWS, HD), jnp.float32),
            pltpu.VMEM((PAD_BLOCKS * BLOCK, HD), jnp.bfloat16),
            pltpu.VMEM((PAD_BLOCKS * BLOCK, HD), jnp.bfloat16),
            pltpu.VMEM((HD, PAD_BLOCKS * BLOCK), jnp.bfloat16),
            pltpu.VMEM((PAD_BLOCKS * BLOCK, HD), jnp.float32),
            pltpu.VMEM((PAD_BLOCKS * BLOCK, HD), jnp.float32),
            pltpu.VMEM((HALF, HD), jnp.bfloat16),
            pltpu.SemaphoreType.DMA((len(arrays) + 4,)),
        ],
        compiler_params=pltpu.CompilerParams(vmem_limit_bytes=24 * 1024 * 1024),
        name="grads",
    )(meta, *arrays, pltpu.with_memory_space_constraint(other, pltpu.HBM))


def spread(value):
    return lax.all_to_all(value, ("x", "z"), 0, 0, tiled=True)


def swap(value):
    return lax.ppermute(value, "y", [(0, 1), (1, 0)])


def tables(doc_ids, block_order):
    documents, order = doc_ids[0], block_order[0]
    starts = jnp.sum((documents[None, :] < documents[:, None]).astype(jnp.int32), axis=1)
    own_first = jnp.where(
        lax.axis_index("y") == 0,
        order,
        jnp.concatenate([order[OWN_BLOCKS:], order[:OWN_BLOCKS]]),
    )
    table = lax.iota(jnp.int32, ALL_BLOCKS)
    first = jnp.sum(
        jnp.where(own_first[:, None] == table[None, :], starts[None, :], 0), axis=1
    )
    length = (own_first - first)[:OWN_BLOCKS] * ALL_BLOCKS + table[:OWN_BLOCKS]
    rank = jnp.sum((length[None, :] > length[:, None]).astype(jnp.int32), axis=1)
    visits = jnp.sum(
        jnp.where(rank[None, :] == table[:, None], table[None, :OWN_BLOCKS], 0), axis=1
    )
    return jnp.stack([own_first, first, visits])


def to_rows(by_head):
    return by_head.transpose(1, 0, 2).reshape(1, ROWS, HEADS * HD)


def plan(groups, ready_first, queries, keys, values, out_grad, outputs, doc_ids, block_order):
    named = {"q": queries[0], "k": keys[0], "v": values[0], "g": out_grad[0]}
    shift = jnp.reshape((lax.axis_index("z") * ROWS) % BLOCK, (1,)).astype(jnp.int32)
    meta = tables(doc_ids, block_order)
    packed = [
        pack(shift, [named[name] for name in names], outputs[0] if "g" in names else None)
        for names in groups
    ]
    if ready_first:
        packed, meta = lax.optimization_barrier((packed, meta))
    arrays = [spread(group) for group in packed]
    other = swap(arrays[0][:, : 2 * ROWS])
    query_grad, own_grad, other_grad = grads(groups, meta, arrays, other)
    arrived = swap(other_grad)
    query_back = spread(query_grad)
    pair_grad = (own_grad + arrived.astype(jnp.float32)).astype(jnp.bfloat16)
    pair_back = spread(pair_grad)
    return (
        to_rows(query_back),
        to_rows(pair_back[:, :ROWS]),
        to_rows(pair_back[:, ROWS:]),
    )


def local(*arrays):
    return lax.cond(
        lax.axis_index("outer") % 2 == 0,
        functools.partial(plan, CORE0_GROUPS, CORE0_READY),
        functools.partial(plan, CORE1_GROUPS, CORE1_READY),
        *arrays,
    )


def solution(mesh):
    grid = Mesh(mesh.devices.reshape(8, 4, 2, 4), ("z", "outer", "y", "x"))
    rows = P("outer", ("y", "x", "z"), None)
    whole = P("outer", None)
    return jax.shard_map(
        local,
        mesh=grid,
        in_specs=(rows, rows, rows, rows, rows, whole, whole),
        out_specs=(rows, rows, rows),
        check_vma=False,
    )
```

time: 137 us -> 116 us (0.85)
  waiting for transfers between devices: 76.6 us -> 42.8 us
  blocking collectives: 0 us -> 29.1 us
  starting transfers between devices: 32.1 us -> 20.9 us
  Pallas kernels: 18.2 us -> 13.9 us
  other arithmetic: 1.6 us -> 3.95 us
  local copies, waits for them, and re-layouts: 5.95 us -> 3.94 us
    all_to_all x4 -> x3, waiting for transfers between devices: 66.5 us -> 37.1 us  [spread(): return lax.all_to_all(value, ('x', 'z'), 0, 0, tiled=True)]
    all_to_all x0 -> x1, blocking collectives: none -> 29.1 us  [spread(): return lax.all_to_all(value, ('x', 'z'), 0, 0, tiled=True)]
    all_to_all x4 -> x3, starting transfers between devices: 25.8 us -> 15.7 us  [spread(): return lax.all_to_all(value, ('x', 'z'), 0, 0, tiled=True)]
    ppermute x2, waiting for transfers between devices: 10.2 us -> 5.65 us  [swap(): return lax.ppermute(value, 'y', [(0, 1), (1, 0)])]
    pallas_call x3, Pallas kernels: 18.2 us -> 13.9 us  [the longest x1 10.3 us: grads(): pl.pallas_call(functools.partial(grads_kernel, groups), out_shape=(pltpu....]
    unnamed x10 -> x0, local copies, waits for them, and re-layouts: 2.78 us -> none
  transfers between devices with their start and end apart: 6 -> 5, of which waited for: 5 -> 4; matrix products, arithmetic and copies ran while one was open for 2% -> 2% of each run, Pallas kernels for 2% -> 0%
where the time goes in v2:
time: 116 us; the launch traced here: 115 us
  waiting for transfers between devices  42.8 us (37%)
  blocking collectives  29.1 us (25%)
  starting transfers between devices  20.9 us (18%)
  Pallas kernels  13.9 us (12%)
  other arithmetic  3.95 us (3%)
  local copies, waits for them, and re-layouts  3.94 us (3%)
    all_to_all x3, waiting for transfers between devices, spread(): return lax.all_to_all(value, ('x', 'z'), 0, 0, tiled=True)  37.1 us
    all_to_all x1, blocking collectives, spread(): return lax.all_to_all(value, ('x', 'z'), 0, 0, tiled=True)  29.1 us
    all_to_all x3, starting transfers between devices, spread(): return lax.all_to_all(value, ('x', 'z'), 0, 0, tiled=True)  15.7 us
    pallas_call x1, Pallas kernels, grads(): pl.pallas_call(functools.partial(grads_kernel, groups), out_shape=(pltpu....  10.3 us
    ppermute x2, waiting for transfers between devices, swap(): return lax.ppermute(value, 'y', [(0, 1), (1, 0)])  5.65 us
    ppermute x2, starting transfers between devices, swap(): return lax.ppermute(value, 'y', [(0, 1), (1, 0)])  5.2 us
    pallas_call x2, Pallas kernels, pack(): pl.pallas_call(functools.partial(pack_kernel, with_dots), out_shape=jax.S...  3.62 us
    reshape x3, local copies, waits for them, and re-layouts, to_rows(): return by_head.transpose(1, 0, 2).reshape(1, ROWS, HEADS * HD)  2.74 us
  transfers between devices with their start and end apart: 5, of which 4 were waited for; matrix products, arithmetic and copies ran while one was open for 2% of the time, Pallas kernels for 0%

profile of v2, /device:TPU:32, one launch (start us, length us, event | category | flops | bytes accessed | tf_op | source)
XLA Modules:
  0.0 115.5 jit_solution(18255292636938073628)
XLA Ops:
  0.6 114.8 %conditional.1 = (bf16[1,48,4096]{2,1,0:T(8,128)(2,1)}, bf16[1,48,4096]{2,1,0:T(8,128)(2,1)}, bf16[1,48,4096]{2,1,0:T(8,128)(2,1)}) conditional(s32[]{:T(128)} %convert_element_type.27, (s32[1,24]{1,0:T(1,128)}, s32[1,24]{1,0:T(1,128)}, bf16[1,48,4096]{2,1,0:T(8,128)(2,1)}, bf16[1,48,4096]{2,1,0:T(8,128)(2,1)}, bf16[1,48,4096]{2,1,0:T(8,128)(2,1)}, ...), branch_computations={%region_0.5_spmd, %region_5.10_spmd} | conditional | flops 1184623 | bytes 31263964 | solution.py:317
  0.8 0.0 copy-start.2
  0.9 0.0 copy-start.4
  0.9 0.0 copy-start.6
  0.9 0.9 convert_reduce_fusion.2
  1.8 0.8 fusion.1
  2.6 0.7 broadcast_select_fusion.2
  3.4 0.2 select_reduce_fusion.2
  3.6 0.2 convert_reduce_fusion.3
  3.8 0.7 broadcast_select_fusion.3
  4.5 0.1 select_reduce_fusion.3
  4.6 2.2 %pack.6 = bf16[32,96,128]{2,1,0:T(8,128)(2,1)} custom-call(s32[1]{0:T(128)} %bitcast.15.shift_ref, bf16[48,4096]{1,0:T(8,128)(2,1)} %bitcast.49, bf16[48,4096]{1,0:T(8,128)(2,1)} %bitcast.51), custom_call_target="tpu_custom_call" | custom-call | tf_op jit(solution)/shard_map/cond/branch_1_fun/pack/pallas_call | solution.py:74
  6.8 0.0 copy-start
  6.8 0.0 copy-done.2
  6.8 0.0 copy-done.4
  6.8 0.0 copy-done.6
  6.8 1.5 %pack.7 = bf16[32,104,128]{2,1,0:T(8,128)(2,1)} custom-call(s32[1]{0:T(128)} %bitcast.15.shift_ref, bf16[48,4096]{1,0:T(8,128)(2,1)S(1)} %bitcast.41, bf16[48,4096]{1,0:T(8,128)(2,1)S(1)} %bitcast.43, bf16[48,4096]{1,0:T(8,128)(2,1)S(1)} %bitcast.45), custom_call_target="tpu_custom_call" | custom-call | tf_op jit(solution)/shard_map/cond/branch_1_fun/pack/pallas_call | solution.py:74
  8.2 0.0 copy-done
  8.3 29.1 %all_to_all.32.refs_0_ = bf16[32,96,128]{2,1,0:T(8,128)(2,1)S(1)} all-to-all(bf16[32,96,128]{2,1,0:T(8,128)(2,1)S(1)} %copy-done), channel_id=1, replica_groups=mesh['z'=8,'outer'=4,'y'=2,'x'=4] {'x','z'}, dimensions={0} | all-to-all | bytes 1572864 | tf_op jit(solution)/shard_map/cond/branch_1_fun/all_to_all | solution.py:261
  37.3 4.9 %all-to-all-start.5 = ((bf16[32,104,128]{2,1,0:T(8,128)(2,1)}), bf16[32,104,128]{2,1,0:T(8,128)(2,1)S(1)}, u32[]{:S(2)}, u32[]{:S(2)}) async-start(bf16[32,104,128]{2,1,0:T(8,128)(2,1)} %pack.7), calls=%async_computation.5 | async-start | bytes 1703936 | tf_op jit(solution)/shard_map/cond/branch_1_fun/all_to_all | solution.py:261
  42.3 3.3 %collective-permute-start.2 = (bf16[32,96,128]{2,1,0:T(8,128)(2,1)S(1)}, bf16[32,96,128]{2,1,0:T(8,128)(2,1)}, u32[]{:S(2)}, u32[]{:S(2)}) collective-permute-start(bf16[32,96,128]{2,1,0:T(8,128)(2,1)S(1)} %all_to_all.32.refs_0_), channel_id=1, source_target_pairs={{0,4},{4,0},{1,5},{5,1},{2,6},{6,2},{3,7},{7,3},{8,12},{12,8},{9,1... | collective-permute-start | bytes 2359304 | tf_op jit(solution)/shard_map/cond/branch_1_fun/ppermute | solution.py:265
  45.5 15.5 %all-to-all-done.5.refs_1_ = bf16[32,104,128]{2,1,0:T(8,128)(2,1)S(1)} async-done(((bf16[32,104,128]{2,1,0:T(8,128)(2,1)}), bf16[32,104,128]{2,1,0:T(8,128)(2,1)S(1)}, u32[]{:S(2)}, u32[]{:S(2)}) %all-to-all-start.5) | async-done | bytes 852000 | tf_op jit(solution)/shard_map/cond/branch_1_fun/all_to_all | solution.py:261
  61.1 0.0 collective-permute-done.2.refs_2_
  61.1 10.3 %grads.3 = (bf16[32,48,128]{2,1,0:T(8,128)(2,1)}, f32[32,96,128]{2,1,0:T(8,128)S(1)}, bf16[32,96,128]{2,1,0:T(8,128)(2,1)}) custom-call(s32[3,24]{1,0:T(4,128)S(1)} %pad_add_fusion.1.meta_ref, bf16[32,96,128]{2,1,0:T(8,128)(2,1)S(1)} %all_to_all.32.refs_0_, bf16[32,104,128]{2,1,0:T(8,128)(2,1)S(1)} %all-to-all-done.5.refs_1_, ...), custom_call_target="tpu_custom_call" | custom-call | tf_op jit(solution)/shard_map/cond/branch_1_fun/grads/pallas_call | solution.py:229
  71.4 1.9 %collective-permute-start.3 = (bf16[32,96,128]{2,1,0:T(8,128)(2,1)}, bf16[32,96,128]{2,1,0:T(8,128)(2,1)S(1)}, u32[]{:S(2)}, u32[]{:S(2)}) collective-permute-start(bf16[32,96,128]{2,1,0:T(8,128)(2,1)} %get-tuple-element.50), channel_id=1, source_target_pairs={{0,4},{4,0},{1,5},{5,1},{2,6},{6,2},{3,7},{7,3},{8,12},{12,8},{9,1... | collective-permute-start | bytes 2359304 | tf_op jit(solution)/shard_map/cond/branch_1_fun/ppermute | solution.py:265
  73.3 6.2 %all-to-all-start.6 = ((bf16[32,48,128]{2,1,0:T(8,128)(2,1)}), bf16[32,48,128]{2,1,0:T(8,128)(2,1)S(1)}, u32[]{:S(2)}, u32[]{:S(2)}) async-start(bf16[32,48,128]{2,1,0:T(8,128)(2,1)} %get-tuple-element.48), calls=%async_computation.6 | async-start | bytes 786432 | tf_op jit(solution)/shard_map/cond/branch_1_fun/all_to_all | solution.py:261
  79.5 5.6 %collective-permute-done.3 = bf16[32,96,128]{2,1,0:T(8,128)(2,1)S(1)} collective-permute-done((bf16[32,96,128]{2,1,0:T(8,128)(2,1)}, bf16[32,96,128]{2,1,0:T(8,128)(2,1)S(1)}, u32[]{:S(2)}, u32[]{:S(2)}) %collective-permute-start.3) | collective-permute-done | bytes 786464 | tf_op jit(solution)/shard_map/cond/branch_1_fun/ppermute | solution.py:265
  85.1 1.1 add_convert_fusion.1
  86.2 5.6 %all-to-all-done.6 = bf16[32,48,128]{2,1,0:T(8,128)(2,1)S(1)} async-done(((bf16[32,48,128]{2,1,0:T(8,128)(2,1)}), bf16[32,48,128]{2,1,0:T(8,128)(2,1)S(1)}, u32[]{:S(2)}, u32[]{:S(2)}) %all-to-all-start.6) | async-done | bytes 393248 | tf_op jit(solution)/shard_map/cond/branch_1_fun/all_to_all | solution.py:261
  91.8 4.5 %all-to-all-start.7 = ((bf16[32,96,128]{2,1,0:T(8,128)(2,1)}), bf16[32,96,128]{2,1,0:T(8,128)(2,1)S(1)}, u32[]{:S(2)}, u32[]{:S(2)}) async-start(bf16[32,96,128]{2,1,0:T(8,128)(2,1)} %add_convert_fusion.1), calls=%async_computation.7 | async-start | bytes 1572864 | tf_op jit(solution)/shard_map/cond/branch_1_fun/all_to_all | solution.py:261
  96.4 0.1 copy.25
  96.5 0.9 reshape.93
  97.4 16.0 %all-to-all-done.7 = bf16[32,96,128]{2,1,0:T(8,128)(2,1)S(1)} async-done(((bf16[32,96,128]{2,1,0:T(8,128)(2,1)}), bf16[32,96,128]{2,1,0:T(8,128)(2,1)S(1)}, u32[]{:S(2)}, u32[]{:S(2)}) %all-to-all-start.7) | async-done | bytes 786464 | tf_op jit(solution)/shard_map/cond/branch_1_fun/all_to_all | solution.py:261
  113.4 0.1 slice_bitcast_fusion.4
  113.4 0.1 copy.27
  113.5 0.9 reshape.95
  114.4 0.1 copy.26
  114.6 0.9 reshape.94
  (4 shorter events, 0.0 us)
Async XLA Ops:
  0.8 5.9 %copy-start.2 = (bf16[1,48,4096]{2,1,0:T(8,128)(2,1)S(1)}, bf16[1,48,4096]{2,1,0:T(8,128)(2,1)}, u32[]{:S(2)}) copy-start(bf16[1,48,4096]{2,1,0:T(8,128)(2,1)} %get-tuple-element.40) | copy-start | bytes 1179652 | tf_op jit(solution)/shard_map/cond
  0.9 5.9 %copy-start.4 = (bf16[1,48,4096]{2,1,0:T(8,128)(2,1)S(1)}, bf16[1,48,4096]{2,1,0:T(8,128)(2,1)}, u32[]{:S(2)}) copy-start(bf16[1,48,4096]{2,1,0:T(8,128)(2,1)} %get-tuple-element.41) | copy-start | bytes 1179652 | tf_op jit(solution)/shard_map/cond
  0.9 5.9 %copy-start.6 = (bf16[1,48,4096]{2,1,0:T(8,128)(2,1)S(1)}, bf16[1,48,4096]{2,1,0:T(8,128)(2,1)}, u32[]{:S(2)}) copy-start(bf16[1,48,4096]{2,1,0:T(8,128)(2,1)} %get-tuple-element.42) | copy-start | bytes 1179652 | tf_op jit(solution)/shard_map/cond
  6.8 1.5 %copy-start = (bf16[32,96,128]{2,1,0:T(8,128)(2,1)S(1)}, bf16[32,96,128]{2,1,0:T(8,128)(2,1)}, u32[]{:S(2)}) copy-start(bf16[32,96,128]{2,1,0:T(8,128)(2,1)} %pack.6) | copy-start | bytes 2359300 | tf_op jit(solution)/shard_map/cond
  37.3 23.7 %all-to-all-start.5 = ((bf16[32,104,128]{2,1,0:T(8,128)(2,1)}), bf16[32,104,128]{2,1,0:T(8,128)(2,1)S(1)}, u32[]{:S(2)}, u32[]{:S(2)}) async-start(bf16[32,104,128]{2,1,0:T(8,128)(2,1)} %pack.7), calls=%async_computation.5 | async-start | bytes 1703936 | tf_op jit(solution)/shard_map/cond/branch_1_fun/all_to_all | solution.py:261
  42.3 18.8 %collective-permute-start.2 = (bf16[32,96,128]{2,1,0:T(8,128)(2,1)S(1)}, bf16[32,96,128]{2,1,0:T(8,128)(2,1)}, u32[]{:S(2)}, u32[]{:S(2)}) collective-permute-start(bf16[32,96,128]{2,1,0:T(8,128)(2,1)S(1)} %all_to_all.32.refs_0_), channel_id=1, source_target_pairs={{0,4},{4,0},{1,5},{5,1},{2,6},{6,2},{3,7},{7,3},{8,12},{12,8},{9,1... | collective-permute-start | bytes 2359304 | tf_op jit(solution)/shard_map/cond/branch_1_fun/ppermute | solution.py:265
  71.4 13.8 %collective-permute-start.3 = (bf16[32,96,128]{2,1,0:T(8,128)(2,1)}, bf16[32,96,128]{2,1,0:T(8,128)(2,1)S(1)}, u32[]{:S(2)}, u32[]{:S(2)}) collective-permute-start(bf16[32,96,128]{2,1,0:T(8,128)(2,1)} %get-tuple-element.50), channel_id=1, source_target_pairs={{0,4},{4,0},{1,5},{5,1},{2,6},{6,2},{3,7},{7,3},{8,12},{12,8},{9,1... | collective-permute-start | bytes 2359304 | tf_op jit(solution)/shard_map/cond/branch_1_fun/ppermute | solution.py:265
  73.3 18.6 %all-to-all-start.6 = ((bf16[32,48,128]{2,1,0:T(8,128)(2,1)}), bf16[32,48,128]{2,1,0:T(8,128)(2,1)S(1)}, u32[]{:S(2)}, u32[]{:S(2)}) async-start(bf16[32,48,128]{2,1,0:T(8,128)(2,1)} %get-tuple-element.48), calls=%async_computation.6 | async-start | bytes 786432 | tf_op jit(solution)/shard_map/cond/branch_1_fun/all_to_all | solution.py:261
  91.8 21.5 %all-to-all-start.7 = ((bf16[32,96,128]{2,1,0:T(8,128)(2,1)}), bf16[32,96,128]{2,1,0:T(8,128)(2,1)S(1)}, u32[]{:S(2)}, u32[]{:S(2)}) async-start(bf16[32,96,128]{2,1,0:T(8,128)(2,1)} %add_convert_fusion.1), calls=%async_computation.7 | async-start | bytes 1572864 | tf_op jit(solution)/shard_map/cond/branch_1_fun/all_to_all | solution.py:261

commit v3 on v2

--- a/solution.py
+++ b/solution.py
@@ -24,10 +24,10 @@
 SCALE_LOG2 = SCALE * math.log2(math.e)
 NEG_FILL = -1e30
 GROUP = 4
-WINDOWS = (2, 4, 8, 12)
-
-CORE0_GROUPS, CORE0_READY = (("k", "v"), ("q", "g")), True
-CORE1_GROUPS, CORE1_READY = (("k", "v"), ("q", "g")), False
+WINDOWS = (2, 4, 6, 8, 12)
+TOGETHER = (4, 8, 12)
+
+GROUPS = (("k", "v"), ("q", "g"))
 
 CONTRACT_LAST = (((1,), (1,)), ((), ()))
 
@@ -108,9 +108,11 @@
     keyt_s[:, tail:] = jnp.zeros((HD, PAD_ROWS), jnp.bfloat16)
     key_acc[...] = jnp.zeros(key_acc.shape, jnp.float32)
     value_acc[...] = jnp.zeros(value_acc.shape, jnp.float32)
-    for load in loads:
+    for load in loads[:-1]:
         load.wait()
     for side, names in ((0, ("k", "v")), (1, ("other_k", "other_v"))):
+        if side == 1:
+            loads[-1].wait()
         keys, values = rows(names[0]), rows(names[1])
         for block in range(OWN_BLOCKS):
             stored = slice(block * BLOCK, (block + 1) * BLOCK)
@@ -137,64 +139,83 @@
         for index in range(3):
             dot_s[3 * group + index : 3 * group + index + 1, :] = blocks[index]
 
-    def visit(blocks, width):
+    def block_weights(block, ahead, scores, weight_grad):
+        reach = (meta_ref[0, block] - meta_ref[1, block]) * BLOCK
+        scores = jnp.where(ahead <= reach, scores, NEG_FILL)
+        highest = jnp.max(scores, axis=0, keepdims=True)
+        weights = jnp.exp2((scores - highest) * SCALE_LOG2)
+        weights = weights * (1.0 / jnp.sum(weights, axis=0, keepdims=True))
+        score_grad = weights * (weight_grad - dot_s[pl.ds(block, 1), :])
+        return weights.astype(jnp.bfloat16), score_grad.astype(jnp.bfloat16)
+
+    def visit(blocks, width, parts):
         shape = (width * BLOCK, BLOCK)
         ahead = lax.broadcasted_iota(jnp.int32, shape, 0) - lax.broadcasted_iota(
             jnp.int32, shape, 1
         )
-        places, scores, weight_grads = [], [], []
-        for block in blocks:
-            first = meta_ref[1, block]
-            rows = pl.ds(pl.multiple_of(block * BLOCK, BLOCK), BLOCK)
-            span = pl.ds(pl.multiple_of(first * BLOCK, BLOCK), width * BLOCK)
-            places.append((block, rows, span))
-            score = lax.dot_general(
-                key_s[span, :],
-                query_s[rows, :],
-                CONTRACT_LAST,
-                preferred_element_type=jnp.float32,
+        found = []
+        for part in parts:
+            members = [blocks[index] for index in part]
+            places = [
+                pl.ds(pl.multiple_of(block * BLOCK, BLOCK), BLOCK) for block in members
+            ]
+            first = pl.multiple_of(meta_ref[1, members[0]] * BLOCK, BLOCK)
+            span = pl.ds(first, width * BLOCK)
+            query = jnp.concatenate([query_s[rows, :] for rows in places], axis=0)
+            grad = jnp.concatenate([grad_s[rows, :] for rows in places], axis=0)
+            scores = lax.dot_general(
+                key_s[span, :], query, CONTRACT_LAST, preferred_element_type=jnp.float32
             )
-            reach = (meta_ref[0, block] - first) * BLOCK
-            scores.append(jnp.where(ahead <= reach, score, NEG_FILL))
-            weight_grads.append(
-                lax.dot_general(
-                    value_s[span, :],
-                    grad_s[rows, :],
-                    CONTRACT_LAST,
-                    preferred_element_type=jnp.float32,
+            weight_grads = lax.dot_general(
+                value_s[span, :], grad, CONTRACT_LAST, preferred_element_type=jnp.float32
+            )
+            found.append((members, places, span, query, grad, scores, weight_grads))
+        rounded = []
+        for members, _, _, _, _, scores, weight_grads in found:
+            pairs = [
+                block_weights(
+                    block,
+                    ahead,
+                    scores[:, index * BLOCK : (index + 1) * BLOCK],
+                    weight_grads[:, index * BLOCK : (index + 1) * BLOCK],
                 )
-                - dot_s[pl.ds(block, 1), :]
-            )
-        lows, score_grads = [], []
-        for score, weight_grad in zip(scores, weight_grads):
-            highest = jnp.max(score, axis=0, keepdims=True)
-            weights = jnp.exp2((score - highest) * SCALE_LOG2)
-            weights = weights * (1.0 / jnp.sum(weights, axis=0, keepdims=True))
-            lows.append(weights.astype(jnp.bfloat16))
-            score_grads.append((weights * weight_grad).astype(jnp.bfloat16))
-        value_parts, key_parts = [], []
-        for (_, rows, span), low, score_grad in zip(places, lows, score_grads):
-            value_parts.append(jnp.dot(low, grad_s[rows, :], preferred_element_type=jnp.float32))
-            key_parts.append(
-                jnp.dot(score_grad, query_s[rows, :], preferred_element_type=jnp.float32)
-            )
+                for index, block in enumerate(members)
+            ]
+            rounded.append([jnp.concatenate(column, axis=1) for column in zip(*pairs)])
+        sums = []
+        for (_, places, span, query, grad, _, _), (low, score_grad) in zip(found, rounded):
+            value_part = jnp.dot(low, grad, preferred_element_type=jnp.float32)
+            key_part = jnp.dot(score_grad, query, preferred_element_type=jnp.float32)
             turned = jnp.dot(keyt_s[:, span], score_grad, preferred_element_type=jnp.float32)
-            dq_s[rows, :] = (turned.T * SCALE).astype(jnp.bfloat16)
-        for (_, _, span), value_part, key_part in zip(places, value_parts, key_parts):
+            for index, rows in enumerate(places):
+                columns = slice(index * BLOCK, (index + 1) * BLOCK)
+                dq_s[rows, :] = (turned[:, columns].T * SCALE).astype(jnp.bfloat16)
+            sums.append((span, value_part, key_part))
+        for span, value_part, key_part in sums:
             value_acc[span, :] += value_part
             key_acc[span, :] += key_part
 
     def step(group, carry):
         blocks = [meta_ref[2, group * GROUP + member] for member in range(GROUP)]
-        count = meta_ref[0, blocks[0]] - meta_ref[1, blocks[0]] + 1
-        most = 0
-        for width in WINDOWS:
-
-            @pl.when((count > most) & (count <= width))
-            def _(width=width):
-                visit(blocks, width)
-
-            most = width
+        firsts = [meta_ref[1, block] for block in blocks]
+        counts = [meta_ref[0, block] - first + 1 for block, first in zip(blocks, firsts)]
+        count = functools.reduce(jnp.maximum, counts)
+        alike = functools.reduce(
+            jnp.logical_and, [first == firsts[0] for first in firsts[1:]]
+        )
+        apart = jnp.logical_not(alike)
+        for chosen, widths, parts in (
+            (alike, TOGETHER, (tuple(range(GROUP)),)),
+            (apart, WINDOWS, tuple((member,) for member in range(GROUP))),
+        ):
+            most = 0
+            for width in widths:
+
+                @pl.when(chosen & (count > most) & (count <= width))
+                def _(width=width, parts=parts):
+                    visit(blocks, width, parts)
+
+                most = width
         return carry
 
     lax.fori_loop(0, OWN_BLOCKS // GROUP, step, 0)
@@ -277,7 +298,9 @@
     first = jnp.sum(
         jnp.where(own_first[:, None] == table[None, :], starts[None, :], 0), axis=1
     )
-    length = (own_first - first)[:OWN_BLOCKS] * ALL_BLOCKS + table[:OWN_BLOCKS]
+    sizes = jnp.sum((documents[None, :] == documents[:, None]).astype(jnp.int32), axis=1)
+    size = jnp.sum(jnp.where(own_first[:, None] == table[None, :], sizes[None, :], 0), axis=1)
+    length = (((size * ALL_BLOCKS) + own_first - first) * ALL_BLOCKS + table)[:OWN_BLOCKS]
     rank = jnp.sum((length[None, :] > length[:, None]).astype(jnp.int32), axis=1)
     visits = jnp.sum(
         jnp.where(rank[None, :] == table[:, None], table[None, :OWN_BLOCKS], 0), axis=1
@@ -289,19 +312,26 @@
     return by_head.transpose(1, 0, 2).reshape(1, ROWS, HEADS * HD)
 
 
-def plan(groups, ready_first, queries, keys, values, out_grad, outputs, doc_ids, block_order):
-    named = {"q": queries[0], "k": keys[0], "v": values[0], "g": out_grad[0]}
+def first_leg(ready_first, queries, keys, values, out_grad, outputs, doc_ids, block_order):
     shift = jnp.reshape((lax.axis_index("z") * ROWS) % BLOCK, (1,)).astype(jnp.int32)
     meta = tables(doc_ids, block_order)
-    packed = [
-        pack(shift, [named[name] for name in names], outputs[0] if "g" in names else None)
-        for names in groups
-    ]
+    pair = pack(shift, [keys[0], values[0]])
+    query_parts = pack(shift, [queries[0], out_grad[0]], outputs[0])
     if ready_first:
-        packed, meta = lax.optimization_barrier((packed, meta))
-    arrays = [spread(group) for group in packed]
-    other = swap(arrays[0][:, : 2 * ROWS])
-    query_grad, own_grad, other_grad = grads(groups, meta, arrays, other)
+        pair, query_parts, meta = lax.optimization_barrier((pair, query_parts, meta))
+    return spread(pair), query_parts, meta
+
+
+def local(*arrays):
+    pair, query_parts, meta = lax.cond(
+        lax.axis_index("outer") % 2 == 0,
+        functools.partial(first_leg, True),
+        functools.partial(first_leg, False),
+        *arrays,
+    )
+    query_parts = spread(query_parts)
+    other = swap(pair)
+    query_grad, own_grad, other_grad = grads(GROUPS, meta, [pair, query_parts], other)
     arrived = swap(other_grad)
     query_back = spread(query_grad)
     pair_grad = (own_grad + arrived.astype(jnp.float32)).astype(jnp.bfloat16)
@@ -310,15 +340,6 @@
         to_rows(query_back),
         to_rows(pair_back[:, :ROWS]),
         to_rows(pair_back[:, ROWS:]),
-    )
-
-
-def local(*arrays):
-    return lax.cond(
-        lax.axis_index("outer") % 2 == 0,
-        functools.partial(plan, CORE0_GROUPS, CORE0_READY),
-        functools.partial(plan, CORE1_GROUPS, CORE1_READY),
-        *arrays,
     )
 
 

time: 116 us -> 116 us (level)
  Pallas kernels: 13.9 us -> 12.5 us
  starting transfers between devices: 20.9 us -> 22.2 us
    all_to_all x3, waiting for transfers between devices: 37.1 us -> 25.1 us  [spread(): return lax.all_to_all(value, ('x', 'z'), 0, 0, tiled=True)]
    ppermute x2, waiting for transfers between devices: 5.65 us -> 17.5 us  [swap(): return lax.ppermute(value, 'y', [(0, 1), (1, 0)])]
    ppermute x2, starting transfers between devices: 5.2 us -> 6.77 us  [swap(): return lax.ppermute(value, 'y', [(0, 1), (1, 0)])]
    pallas_call x1, Pallas kernels: 10.3 us -> 8.91 us  [grads(): pl.pallas_call(functools.partial(grads_kernel, groups), out_shape=(pltpu....]
  transfers between devices with their start and end apart: 5 -> 5, of which waited for: 4 -> 5; matrix products, arithmetic and copies ran while one was open for 2% -> 2% of each run, Pallas kernels for 0% -> 0%
where the time goes in v3:
time: 116 us; the launch traced here: 115 us
  waiting for transfers between devices  42.6 us (37%)
  blocking collectives  29.2 us (25%)
  starting transfers between devices  22.2 us (19%)
  Pallas kernels  12.5 us (11%)
  local copies, waits for them, and re-layouts  3.94 us (3%)
  other arithmetic  3.94 us (3%)
    all_to_all x1, blocking collectives, spread(): return lax.all_to_all(value, ('x', 'z'), 0, 0, tiled=True)  29.2 us
    all_to_all x3, waiting for transfers between devices, spread(): return lax.all_to_all(value, ('x', 'z'), 0, 0, tiled=True)  25.1 us
    ppermute x2, waiting for transfers between devices, swap(): return lax.ppermute(value, 'y', [(0, 1), (1, 0)])  17.5 us
    all_to_all x3, starting transfers between devices, spread(): return lax.all_to_all(value, ('x', 'z'), 0, 0, tiled=True)  15.4 us
    pallas_call x1, Pallas kernels, grads(): pl.pallas_call(functools.partial(grads_kernel, groups), out_shape=(pltpu....  8.91 us
    ppermute x2, starting transfers between devices, swap(): return lax.ppermute(value, 'y', [(0, 1), (1, 0)])  6.77 us
    pallas_call x2, Pallas kernels, pack(): pl.pallas_call(functools.partial(pack_kernel, with_dots), out_shape=jax.S...  3.58 us
    reshape x3, local copies, waits for them, and re-layouts, to_rows(): return by_head.transpose(1, 0, 2).reshape(1, ROWS, HEADS * HD)  2.74 us
  transfers between devices with their start and end apart: 5, of which 5 were waited for; matrix products, arithmetic and copies ran while one was open for 2% of the time, Pallas kernels for 0%

profile of v3, /device:TPU:32, one launch (start us, length us, event | category | flops | bytes accessed | tf_op | source)
XLA Modules:
  0.0 115.2 jit_solution(1471111296811020751)
XLA Ops:
  0.6 36.6 %conditional.1 = (bf16[32,96,128]{2,1,0:T(8,128)(2,1)S(1)}, bf16[32,104,128]{2,1,0:T(8,128)(2,1)}, s32[3,24]{1,0:T(4,128)S(1)}) conditional(s32[]{:T(128)} %convert_element_type.27, (bf16[1,48,4096]{2,1,0:T(8,128)(2,1)}, bf16[1,48,4096]{2,1,0:T(8,128)(2,1)}, bf16[1,48,4096]{2,1,0:T(8,128)(2,1)}, bf16[1,48,4096]{2,1,0:T(8,128)(2,1)}, ...), branch_computations={%region_0.7_spmd, %region_7.14_spmd} | conditional | flops 7879 | bytes 9440492 | solution.py:326
  0.7 0.0 copy-start.2
  0.7 0.0 copy-start.4
  0.7 0.0 copy-start.6
  0.7 0.9 convert_reduce_fusion.3
  1.7 0.8 fusion.1
  2.5 0.7 broadcast_select_fusion.2
  3.2 0.2 select_reduce_fusion.3
  3.4 0.2 convert_reduce_fusion.5
  3.6 0.7 broadcast_select_fusion.3
  4.3 0.1 select_reduce_fusion.5
  4.4 2.1 %pack.6 = bf16[32,96,128]{2,1,0:T(8,128)(2,1)} custom-call(s32[1]{0:T(128)} %bitcast.12.shift_ref, bf16[48,4096]{1,0:T(8,128)(2,1)} %bitcast.47, bf16[48,4096]{1,0:T(8,128)(2,1)} %bitcast.49), custom_call_target="tpu_custom_call" | custom-call | tf_op jit(solution)/shard_map/cond/branch_1_fun/pack/pallas_call | solution.py:74
  6.6 0.0 copy-start
  6.6 0.0 copy-done.2
  6.6 0.0 copy-done.4
  6.6 0.0 copy-done.6
  6.6 1.4 %pack.7 = bf16[32,104,128]{2,1,0:T(8,128)(2,1)} custom-call(s32[1]{0:T(128)} %bitcast.12.shift_ref, bf16[48,4096]{1,0:T(8,128)(2,1)S(1)} %bitcast.40, bf16[48,4096]{1,0:T(8,128)(2,1)S(1)} %bitcast.42, bf16[48,4096]{1,0:T(8,128)(2,1)S(1)} %bitcast.44), custom_call_target="tpu_custom_call" | custom-call | tf_op jit(solution)/shard_map/cond/branch_1_fun/pack/pallas_call | solution.py:74
  8.0 0.0 copy-done
  8.0 29.2 %all_to_all.23 = bf16[32,96,128]{2,1,0:T(8,128)(2,1)S(1)} all-to-all(bf16[32,96,128]{2,1,0:T(8,128)(2,1)S(1)} %copy-done), channel_id=1, replica_groups=mesh['z'=8,'outer'=4,'y'=2,'x'=4] {'x','z'}, dimensions={0} | all-to-all | bytes 1572864 | tf_op jit(solution)/shard_map/cond/branch_1_fun/all_to_all | solution.py:282
  37.2 5.1 %all-to-all-start.2 = ((bf16[32,104,128]{2,1,0:T(8,128)(2,1)}), bf16[32,104,128]{2,1,0:T(8,128)(2,1)S(1)}, u32[]{:S(2)}, u32[]{:S(2)}) async-start(bf16[32,104,128]{2,1,0:T(8,128)(2,1)} %get-tuple-element.56), calls=%async_computation.2 | async-start | bytes 1703936 | tf_op jit(solution)/shard_map/all_to_all | solution.py:282
  42.4 3.3 %collective-permute-start = (bf16[32,96,128]{2,1,0:T(8,128)(2,1)S(1)}, bf16[32,96,128]{2,1,0:T(8,128)(2,1)}, u32[]{:S(2)}, u32[]{:S(2)}) collective-permute-start(bf16[32,96,128]{2,1,0:T(8,128)(2,1)S(1)} %get-tuple-element.55.refs_0_), channel_id=1, source_target_pairs={{0,4},{4,0},{1,5},{5,1},{2,6},{6,2},{3,7},{7,3},{8,12},{12,8},{9,1... | collective-permute-start | bytes 2359304 | tf_op jit(solution)/shard_map/ppermute | solution.py:286
  45.7 11.8 %collective-permute-done.refs_2_ = bf16[32,96,128]{2,1,0:T(8,128)(2,1)} collective-permute-done((bf16[32,96,128]{2,1,0:T(8,128)(2,1)S(1)}, bf16[32,96,128]{2,1,0:T(8,128)(2,1)}, u32[]{:S(2)}, u32[]{:S(2)}) %collective-permute-start) | collective-permute-done | bytes 786464 | tf_op jit(solution)/shard_map/ppermute | solution.py:286
  57.5 3.9 %all-to-all-done.2.refs_1_ = bf16[32,104,128]{2,1,0:T(8,128)(2,1)S(1)} async-done(((bf16[32,104,128]{2,1,0:T(8,128)(2,1)}), bf16[32,104,128]{2,1,0:T(8,128)(2,1)S(1)}, u32[]{:S(2)}, u32[]{:S(2)}) %all-to-all-start.2) | async-done | bytes 852000 | tf_op jit(solution)/shard_map/all_to_all | solution.py:282
  61.3 8.9 %grads.1 = (bf16[32,48,128]{2,1,0:T(8,128)(2,1)}, f32[32,96,128]{2,1,0:T(8,128)S(1)}, bf16[32,96,128]{2,1,0:T(8,128)(2,1)}) custom-call(s32[3,24]{1,0:T(4,128)S(1)} %get-tuple-element.54.meta_ref, bf16[32,96,128]{2,1,0:T(8,128)(2,1)S(1)} %get-tuple-element.55.refs_0_, bf16[32,104,128]{2,1,0:T(8,128)(2,1)S(1)} %all-to-all-done.2.refs_1_, ...), custom_call_target="tpu_custom_call" | custom-call | tf_op jit(solution)/shard_map/grads/pallas_call | solution.py:250
  70.3 3.5 %collective-permute-start.1 = (bf16[32,96,128]{2,1,0:T(8,128)(2,1)}, bf16[32,96,128]{2,1,0:T(8,128)(2,1)S(1)}, u32[]{:S(2)}, u32[]{:S(2)}) collective-permute-start(bf16[32,96,128]{2,1,0:T(8,128)(2,1)} %get-tuple-element.59), channel_id=1, source_target_pairs={{0,4},{4,0},{1,5},{5,1},{2,6},{6,2},{3,7},{7,3},{8,12},{12,8},{9,1... | collective-permute-start | bytes 2359304 | tf_op jit(solution)/shard_map/ppermute | solution.py:286
  73.7 5.8 %all-to-all-start.3 = ((bf16[32,48,128]{2,1,0:T(8,128)(2,1)}), bf16[32,48,128]{2,1,0:T(8,128)(2,1)S(1)}, u32[]{:S(2)}, u32[]{:S(2)}) async-start(bf16[32,48,128]{2,1,0:T(8,128)(2,1)} %get-tuple-element.57), calls=%async_computation.3 | async-start | bytes 786432 | tf_op jit(solution)/shard_map/all_to_all | solution.py:282
  79.5 5.7 %collective-permute-done.1 = bf16[32,96,128]{2,1,0:T(8,128)(2,1)S(1)} collective-permute-done((bf16[32,96,128]{2,1,0:T(8,128)(2,1)}, bf16[32,96,128]{2,1,0:T(8,128)(2,1)S(1)}, u32[]{:S(2)}, u32[]{:S(2)}) %collective-permute-start.1) | collective-permute-done | bytes 786464 | tf_op jit(solution)/shard_map/ppermute | solution.py:286
  85.2 1.0 add_convert_fusion
  86.3 5.6 %all-to-all-done.3 = bf16[32,48,128]{2,1,0:T(8,128)(2,1)S(1)} async-done(((bf16[32,48,128]{2,1,0:T(8,128)(2,1)}), bf16[32,48,128]{2,1,0:T(8,128)(2,1)S(1)}, u32[]{:S(2)}, u32[]{:S(2)}) %all-to-all-start.3) | async-done | bytes 393248 | tf_op jit(solution)/shard_map/all_to_all | solution.py:282
  91.8 4.5 %all-to-all-start.4 = ((bf16[32,96,128]{2,1,0:T(8,128)(2,1)}), bf16[32,96,128]{2,1,0:T(8,128)(2,1)S(1)}, u32[]{:S(2)}, u32[]{:S(2)}) async-start(bf16[32,96,128]{2,1,0:T(8,128)(2,1)} %add_convert_fusion), calls=%async_computation.4 | async-start | bytes 1572864 | tf_op jit(solution)/shard_map/all_to_all | solution.py:282
  96.4 0.1 copy.13
  96.5 0.9 reshape.89
  97.4 15.7 %all-to-all-done.4 = bf16[32,96,128]{2,1,0:T(8,128)(2,1)S(1)} async-done(((bf16[32,96,128]{2,1,0:T(8,128)(2,1)}), bf16[32,96,128]{2,1,0:T(8,128)(2,1)S(1)}, u32[]{:S(2)}, u32[]{:S(2)}) %all-to-all-start.4) | async-done | bytes 786464 | tf_op jit(solution)/shard_map/all_to_all | solution.py:282
  113.1 0.1 slice_bitcast_fusion.4
  113.1 0.1 copy.15
  113.2 0.9 reshape.91
  114.1 0.1 copy.14
  114.2 0.9 reshape.90
  (3 shorter events, 0.0 us)
Async XLA Ops:
  0.7 5.9 %copy-start.2 = (bf16[1,48,4096]{2,1,0:T(8,128)(2,1)S(1)}, bf16[1,48,4096]{2,1,0:T(8,128)(2,1)}, u32[]{:S(2)}) copy-start(bf16[1,48,4096]{2,1,0:T(8,128)(2,1)} %get-tuple-element.37) | copy-start | bytes 1179652 | tf_op jit(solution)/shard_map/cond
  0.7 5.9 %copy-start.4 = (bf16[1,48,4096]{2,1,0:T(8,128)(2,1)S(1)}, bf16[1,48,4096]{2,1,0:T(8,128)(2,1)}, u32[]{:S(2)}) copy-start(bf16[1,48,4096]{2,1,0:T(8,128)(2,1)} %get-tuple-element.38) | copy-start | bytes 1179652 | tf_op jit(solution)/shard_map/cond
  0.7 5.9 %copy-start.6 = (bf16[1,48,4096]{2,1,0:T(8,128)(2,1)S(1)}, bf16[1,48,4096]{2,1,0:T(8,128)(2,1)}, u32[]{:S(2)}) copy-start(bf16[1,48,4096]{2,1,0:T(8,128)(2,1)} %get-tuple-element.39) | copy-start | bytes 1179652 | tf_op jit(solution)/shard_map/cond
  6.6 1.5 %copy-start = (bf16[32,96,128]{2,1,0:T(8,128)(2,1)S(1)}, bf16[32,96,128]{2,1,0:T(8,128)(2,1)}, u32[]{:S(2)}) copy-start(bf16[32,96,128]{2,1,0:T(8,128)(2,1)} %pack.6) | copy-start | bytes 2359300 | tf_op jit(solution)/shard_map/cond
  37.2 24.1 %all-to-all-start.2 = ((bf16[32,104,128]{2,1,0:T(8,128)(2,1)}), bf16[32,104,128]{2,1,0:T(8,128)(2,1)S(1)}, u32[]{:S(2)}, u32[]{:S(2)}) async-start(bf16[32,104,128]{2,1,0:T(8,128)(2,1)} %get-tuple-element.56), calls=%async_computation.2 | async-start | bytes 1703936 | tf_op jit(solution)/shard_map/all_to_all | solution.py:282
  42.4 15.1 %collective-permute-start = (bf16[32,96,128]{2,1,0:T(8,128)(2,1)S(1)}, bf16[32,96,128]{2,1,0:T(8,128)(2,1)}, u32[]{:S(2)}, u32[]{:S(2)}) collective-permute-start(bf16[32,96,128]{2,1,0:T(8,128)(2,1)S(1)} %get-tuple-element.55.refs_0_), channel_id=1, source_target_pairs={{0,4},{4,0},{1,5},{5,1},{2,6},{6,2},{3,7},{7,3},{8,12},{12,8},{9,1... | collective-permute-start | bytes 2359304 | tf_op jit(solution)/shard_map/ppermute | solution.py:286
  70.3 15.0 %collective-permute-start.1 = (bf16[32,96,128]{2,1,0:T(8,128)(2,1)}, bf16[32,96,128]{2,1,0:T(8,128)(2,1)S(1)}, u32[]{:S(2)}, u32[]{:S(2)}) collective-permute-start(bf16[32,96,128]{2,1,0:T(8,128)(2,1)} %get-tuple-element.59), channel_id=1, source_target_pairs={{0,4},{4,0},{1,5},{5,1},{2,6},{6,2},{3,7},{7,3},{8,12},{12,8},{9,1... | collective-permute-start | bytes 2359304 | tf_op jit(solution)/shard_map/ppermute | solution.py:286
  73.7 18.1 %all-to-all-start.3 = ((bf16[32,48,128]{2,1,0:T(8,128)(2,1)}), bf16[32,48,128]{2,1,0:T(8,128)(2,1)S(1)}, u32[]{:S(2)}, u32[]{:S(2)}) async-start(bf16[32,48,128]{2,1,0:T(8,128)(2,1)} %get-tuple-element.57), calls=%async_computation.3 | async-start | bytes 786432 | tf_op jit(solution)/shard_map/all_to_all | solution.py:282
  91.8 21.2 %all-to-all-start.4 = ((bf16[32,96,128]{2,1,0:T(8,128)(2,1)}), bf16[32,96,128]{2,1,0:T(8,128)(2,1)S(1)}, u32[]{:S(2)}, u32[]{:S(2)}) async-start(bf16[32,96,128]{2,1,0:T(8,128)(2,1)} %add_convert_fusion), calls=%async_computation.4 | async-start | bytes 1572864 | tf_op jit(solution)/shard_map/all_to_all | solution.py:282
